TPU v7x, 128 devices: a whole 4x4x4 slice. The times are simulated.
128 devices in a mesh: pipe: 2 (over y_lo), expert: 8 (over z, core), dp: 8 (over y_hi, x).
Axes of the slice: x: 4, y: 4 (y_hi: 2, y_lo: 2; y = y_hi * 2 + y_lo), z: 4, core: 2. Of those that a mesh axis runs over, the one named last changes fastest.
Arguments:
- activations: bfloat16 [2, 2, 4096, 4096], P('pipe', None, ('expert', 'dp')), may hold values from -6 to 6
- cotangent: bfloat16 [2, 4096, 4096], P(None, ('expert', 'dp')), may hold values from -6 to 6
- routes: int32 [2, 2, 4096, 2], P('pipe', None, ('expert', 'dp')), may hold values from 0 to 7, all different within a row; in each aligned block of 64 rows (0 to 63, 64 to 127, ..., all dimensions but the last counted through in order) at most 24 rows name the same one
- route_weights: float32 [2, 2, 4096, 2], P('pipe', None, ('expert', 'dp')), may hold values from 0.1 to 1
- placement: int32 [2, 8], P('pipe'), may hold values from 0 to 7, each once within a row
- gate_weight: bfloat16 [2, 8, 4096, 768], P('pipe', 'expert'), may hold values from -0.09375 to 0.09375
- up_weight: bfloat16 [2, 8, 4096, 768], P('pipe', 'expert'), may hold values from -0.09375 to 0.09375
- down_weight: bfloat16 [2, 8, 4096, 768], P('pipe', 'expert'), may hold values from -0.21875 to 0.21875
Outputs:
- input_grads: bfloat16 [2, 2, 4096, 4096], P('pipe', None, ('expert', 'dp'))
- gate_grads: bfloat16 [2, 8, 4096, 768], P('pipe', 'expert', 'dp')
- up_grads: bfloat16 [2, 8, 4096, 768], P('pipe', 'expert', 'dp')
- down_grads: bfloat16 [2, 8, 4096, 768], P('pipe', 'expert', 'dp')
Inputs may be any that keep to these rules, and one draw needn't show every extreme that they name: `routes`: each token's 2 ids differ; among the 64 tokens of one device, section and micro-batch no expert is named more than 24 times, a bound that some block reaches. `placement`: each row is a permutation.
All inputs are finite; a program needn't handle non-finite values.
Results may differ from a plain program's by a relative error of at most 0.017.
Values may be sent and summed in bfloat16 or wider, within the bound.
A program may use at most 128 MiB of HBM per device.

v0:
```python
import jax
import jax.numpy as jnp
from jax import lax
from jax.sharding import PartitionSpec as P


def shifted(value, axis, by):
    peers = lax.axis_size(axis)
    pairs = [(i, i + by) for i in range(peers) if 0 <= i + by < peers]
    return lax.ppermute(value, axis, pairs)


def expert_backward(rows_in, rows_cot, w_gate, w_up, w_down):
    pre_gate = jnp.dot(rows_in, w_gate, preferred_element_type=jnp.float32)
    pre_up = jnp.dot(rows_in, w_up, preferred_element_type=jnp.float32)
    sigmoid_gate = jax.nn.sigmoid(pre_gate)
    active = pre_gate * sigmoid_gate
    hidden = (active * pre_up).astype(jnp.bfloat16)
    grad_hidden = jnp.dot(rows_cot, w_down, preferred_element_type=jnp.float32)
    grad_gate = (
        grad_hidden * pre_up * sigmoid_gate * (1.0 + pre_gate * (1.0 - sigmoid_gate))
    ).astype(jnp.bfloat16)
    grad_up = (grad_hidden * active).astype(jnp.bfloat16)
    grad_rows = (
        jnp.einsum("rf,df->rd", grad_gate, w_gate, preferred_element_type=jnp.float32)
        + jnp.einsum("rf,df->rd", grad_up, w_up, preferred_element_type=jnp.float32)
    ).astype(jnp.bfloat16)
    return (grad_rows, hidden, grad_gate, grad_up)


def dispatch_plan(route_ids, gate_values, inverse, capacity):
    token_count, top_count = route_ids.shape
    expert_count = inverse.shape[0]
    expert_ids = jnp.arange(expert_count, dtype=jnp.int32)
    slot_ids = jnp.sum(jnp.where(route_ids[:, :, None] == expert_ids, inverse, 0), axis=2).reshape(
        -1
    )
    onehot = (slot_ids[:, None] == expert_ids).astype(jnp.int32)
    slot_rank = jnp.sum((jnp.cumsum(onehot, axis=0) - 1) * onehot, axis=1)
    position = slot_ids * capacity + slot_rank
    places = jnp.arange(expert_count * capacity, dtype=jnp.int32)
    landing = position[:, None] == places
    owners = jnp.arange(token_count * top_count, dtype=jnp.int32) // top_count
    token_hit = (owners[:, None] == jnp.arange(token_count, dtype=jnp.int32)).astype(jnp.bfloat16)
    selector = jnp.einsum(
        "as,at->st", landing.astype(jnp.bfloat16), token_hit, preferred_element_type=jnp.float32
    ).astype(jnp.bfloat16)
    slot_scale = jnp.sum(jnp.where(landing, gate_values.reshape(-1)[:, None], 0.0), axis=0)
    return (selector, slot_scale)


def local(
    activations, cotangent, routes, route_weights, placement, gate_weight, up_weight, down_weight
):
    pipe_size = lax.axis_size("pipe")
    expert_size = lax.axis_size("expert")
    data_size = lax.axis_size("dp")
    section_index = lax.axis_index("pipe")
    micro_count = activations.shape[1]
    token_count = activations.shape[2]
    width = activations.shape[3]
    top_count = routes.shape[3]
    expert_count = placement.shape[1]
    local_experts = gate_weight.shape[1]
    hidden_width = gate_weight.shape[3]
    capacity = 3 * token_count * top_count // (2 * expert_count)
    block_rows = local_experts * capacity
    expert_ids = jnp.arange(expert_count, dtype=jnp.int32)
    inverse = jnp.sum(
        jnp.where(placement[0][None, :] == expert_ids[:, None], expert_ids[None, :], 0), axis=1
    )
    tick_count = micro_count + pipe_size - 1
    incoming = jnp.zeros((token_count, width), jnp.bfloat16)
    input_grads = jnp.zeros((micro_count, token_count, width), jnp.bfloat16)
    kept_in = [[]]
    kept_cot = [[]]
    kept_hidden = [[]]
    kept_gate = [[]]
    kept_up = [[]]
    is_last = section_index == pipe_size - 1
    for tick_step in range(tick_count):
        micro_raw = tick_step - (pipe_size - 1 - section_index)
        is_valid = (micro_raw >= 0) & (micro_raw < micro_count)
        micro_index = jnp.clip(micro_raw, 0, micro_count - 1)
        route_ids = lax.dynamic_index_in_dim(routes[0], micro_index, 0, keepdims=False)
        gate_values = lax.dynamic_index_in_dim(route_weights[0], micro_index, 0, keepdims=False)
        selector, slot_scale = dispatch_plan(route_ids, gate_values, inverse, capacity)
        own_cot = lax.dynamic_index_in_dim(cotangent, micro_index, 0, keepdims=False)
        upstream = jnp.where(
            is_last, jnp.where(is_valid, own_cot, jnp.zeros_like(own_cot)), incoming
        )
        scaled = (
            slot_scale[:, None] * jnp.dot(selector, upstream, preferred_element_type=jnp.float32)
        ).astype(jnp.bfloat16)
        scaled = scaled.reshape(expert_size, block_rows, width)
        local_in = lax.dynamic_index_in_dim(activations[0], micro_index, 0, keepdims=False)
        picked = jnp.dot(selector, local_in, preferred_element_type=jnp.float32).astype(
            jnp.bfloat16
        )
        arrived_in = lax.all_to_all(
            picked.reshape(expert_size, block_rows, width),
            "expert",
            split_axis=0,
            concat_axis=0,
            tiled=True,
        )
        arrived_cot = lax.all_to_all(scaled, "expert", split_axis=0, concat_axis=0, tiled=True)
        local_slot = 0
        rows_in = arrived_in.reshape(-1, width)
        rows_cot = arrived_cot.reshape(-1, width)
        grad_rows, hidden, grad_gate, grad_up = expert_backward(
            rows_in,
            rows_cot,
            gate_weight[0, local_slot],
            up_weight[0, local_slot],
            down_weight[0, local_slot],
        )
        results = grad_rows.reshape(expert_size, capacity, width)
        kept_in[local_slot].append(rows_in)
        kept_cot[local_slot].append(rows_cot)
        kept_hidden[local_slot].append(hidden)
        kept_gate[local_slot].append(grad_gate)
        kept_up[local_slot].append(grad_up)
        returned = lax.all_to_all(results, "expert", split_axis=0, concat_axis=0, tiled=True)
        combined = jnp.einsum(
            "st,sd->td", selector, returned.reshape(-1, width), preferred_element_type=jnp.float32
        )
        local_grad = (upstream.astype(jnp.float32) + combined).astype(jnp.bfloat16)
        updated = lax.dynamic_update_index_in_dim(input_grads, local_grad, micro_index, 0)
        input_grads = jnp.where(is_valid, updated, input_grads)
        if tick_step + 1 < tick_count:
            incoming = shifted(local_grad, "pipe", -1)
    all_in = [jnp.concatenate(kept_in[0], axis=0)]
    all_cot = [jnp.concatenate(kept_cot[0], axis=0)]
    all_hidden = [jnp.concatenate(kept_hidden[0], axis=0)]
    all_gate_up = [
        jnp.concatenate(
            [jnp.concatenate(kept_gate[0], axis=0), jnp.concatenate(kept_up[0], axis=0)], axis=1
        )
    ]
    share_rows = width // data_size
    pieces = []
    local_slot = 0
    in_cols = all_in[local_slot]
    cot_cols = all_cot[local_slot]
    pieces.append(
        jnp.einsum(
            "rc,rf->cf", in_cols, all_gate_up[local_slot], preferred_element_type=jnp.float32
        )
    )
    pieces.append(
        jnp.einsum(
            "rc,rf->cf", cot_cols, all_hidden[local_slot], preferred_element_type=jnp.float32
        )
    )
    scattered = lax.psum_scatter(
        jnp.concatenate(pieces, axis=1).astype(jnp.bfloat16), "dp", scatter_dimension=0, tiled=True
    ).astype(jnp.float32)
    scattered = scattered.reshape(share_rows, local_experts, 3, hidden_width)
    weight_grads = jnp.transpose(scattered, (2, 1, 0, 3)).astype(jnp.bfloat16)
    return (input_grads[None], weight_grads[0][None], weight_grads[1][None], weight_grads[2][None])


def solution(mesh):
    placed = (
        P("pipe", None, ("expert", "dp"), None),
        P(None, ("expert", "dp"), None),
        P("pipe", None, ("expert", "dp"), None),
        P("pipe", None, ("expert", "dp"), None),
        P("pipe", None),
        P("pipe", "expert", None, None),
        P("pipe", "expert", None, None),
        P("pipe", "expert", None, None),
    )
    return jax.shard_map(
        local,
        mesh=mesh,
        in_specs=placed,
        out_specs=(
            P("pipe", None, ("expert", "dp"), None),
            P("pipe", "expert", "dp", None),
            P("pipe", "expert", "dp", None),
            P("pipe", "expert", "dp", None),
        ),
        check_vma=False,
    )
```

profile of v0, /device:TPU:1, one launch (start us, length us, event | category | flops | bytes accessed | tf_op | source)
XLA Modules:
  0.0 528.2 jit_solution(16306554891077508992)
XLA Ops:
  13.8 6.8 %all-to-all-start = ((bf16[8,24,4096]{2,1,0:T(8,128)(2,1)}), bf16[8,24,4096]{2,1,0:T(8,128)(2,1)S(1)}, u32[]{:S(2)}, u32[]{:S(2)}) async-start(bf16[8,24,4096]{2,1,0:T(8,128)(2,1)} %bitcast.171), calls=%async_computation | async-start | bytes 3145728 | tf_op jit(solution)/shard_map/all_to_all | solution.py:107
  22.4 18.9 %all-to-all-done = bf16[8,24,4096]{2,1,0:T(8,128)(2,1)S(1)} async-done(((bf16[8,24,4096]{2,1,0:T(8,128)(2,1)}), bf16[8,24,4096]{2,1,0:T(8,128)(2,1)S(1)}, u32[]{:S(2)}, u32[]{:S(2)}) %all-to-all-start) | async-done | bytes 1572896 | tf_op jit(solution)/shard_map/all_to_all | solution.py:107
  41.3 5.0 all-to-all-start.1
  46.3 5.0 fusion.28
  51.3 15.9 %all-to-all-done.1 = bf16[8,24,4096]{2,1,0:T(8,128)(2,1)} async-done(((bf16[8,24,4096]{2,1,0:T(8,128)(2,1)}), bf16[8,24,4096]{2,1,0:T(8,128)(2,1)}, u32[]{:S(2)}, u32[]{:S(2)}) %all-to-all-start.1) | async-done | bytes 1572896 | tf_op jit(solution)/shard_map/all_to_all | solution.py:100
  67.2 4.8 fusion.10
  72.0 5.7 %multiply_convert_fusion.2 = (bf16[192,768]{1,0:T(8,128)(2,1)}, bf16[192,768]{1,0:T(8,128)(2,1)S(1)}, bf16[192,768]{1,0:T(8,128)(2,1)S(1)}) fusion(f32[192,768]{1,0:T(8,128)S(1)} %fusion.10, f32[192,768]{1,0:T(8,128)S(1)} %copy-done.13, bf16[192,4096]{1,0:T(8,128)(2,1)} %bitcast.8, bf16[1,1,4096,768]{3,2,1,0:T(8,128)(2,1)} %param.14), kind=kOutput, calls=%fused_computation.83 | convolution fusion | flops 1210171392 | bytes 9928704 | tf_op jit(solution)/shard_map/dot_general | solution.py:15
  90.4 18.0 %all-to-all-done.2 = bf16[8,24,4096]{2,1,0:T(8,128)(2,1)S(1)} async-done(((bf16[8,24,4096]{2,1,0:T(8,128)(2,1)}), bf16[8,24,4096]{2,1,0:T(8,128)(2,1)S(1)}, u32[]{:S(2)}, u32[]{:S(2)}) %all-to-all-start.2) | async-done | bytes 1572896 | tf_op jit(solution)/shard_map/all_to_all | solution.py:124
  108.4 5.0 all-to-all-start.4
  118.0 13.9 %collective-permute-done = bf16[64,4096]{1,0:T(8,128)(2,1)S(1)} collective-permute-done((bf16[64,4096]{1,0:T(8,128)(2,1)}, bf16[64,4096]{1,0:T(8,128)(2,1)S(1)}, u32[]{:S(2)}, u32[]{:S(2)}) %collective-permute-start) | collective-permute-done | bytes 524320 | tf_op jit(solution)/shard_map/ppermute | solution.py:10
  134.7 5.8 %all-to-all-start.3 = ((bf16[8,24,4096]{2,1,0:T(8,128)(2,1)}), bf16[8,24,4096]{2,1,0:T(8,128)(2,1)}, u32[]{:S(2)}, u32[]{:S(2)}) async-start(bf16[8,24,4096]{2,1,0:T(8,128)(2,1)} %bitcast.170), calls=%async_computation.3 | async-start | bytes 3145728 | tf_op jit(solution)/shard_map/all_to_all | solution.py:107
  140.5 5.5 %fusion.6 = f32[192,768]{1,0:T(8,128)} fusion(bf16[192,4096]{1,0:T(8,128)(2,1)} %bitcast.20, bf16[1,1,4096,768]{3,2,1,0:T(8,128)(2,1)} %param.13), kind=kOutput, calls=%fused_computation.9 | convolution fusion | flops 1207959552 | bytes 8454144 | tf_op jit(solution)/shard_map/dot_general | solution.py:14
  146.0 15.3 %all-to-all-done.3 = bf16[8,24,4096]{2,1,0:T(8,128)(2,1)} async-done(((bf16[8,24,4096]{2,1,0:T(8,128)(2,1)}), bf16[8,24,4096]{2,1,0:T(8,128)(2,1)}, u32[]{:S(2)}, u32[]{:S(2)}) %all-to-all-start.3) | async-done | bytes 1572896 | tf_op jit(solution)/shard_map/all_to_all | solution.py:107
  161.3 4.8 fusion.26
  166.1 5.7 %multiply_convert_fusion.1 = (bf16[192,768]{1,0:T(8,128)(2,1)}, bf16[192,768]{1,0:T(8,128)(2,1)S(1)}, bf16[192,768]{1,0:T(8,128)(2,1)S(1)}) fusion(f32[192,768]{1,0:T(8,128)S(1)} %copy-done.14, f32[192,768]{1,0:T(8,128)S(1)} %fusion.26, bf16[192,4096]{1,0:T(8,128)(2,1)} %bitcast.20, bf16[1,1,4096,768]{3,2,1,0:T(8,128)(2,1)} %param.14), kind=kOutput, calls=%fused_computation.82 | convolution fusion | flops 1210171392 | bytes 9928704 | tf_op jit(solution)/shard_map/dot_general | solution.py:15
  177.4 5.0 all-to-all-start.5
  185.2 18.1 %all-to-all-done.5 = bf16[8,24,4096]{2,1,0:T(8,128)(2,1)} async-done(((bf16[8,24,4096]{2,1,0:T(8,128)(2,1)}), bf16[8,24,4096]{2,1,0:T(8,128)(2,1)}, u32[]{:S(2)}, u32[]{:S(2)}) %all-to-all-start.5) | async-done | bytes 1572896 | tf_op jit(solution)/shard_map/all_to_all | solution.py:124
  203.3 5.0 all-to-all-start.7
  212.1 13.6 %collective-permute-done.1 = bf16[64,4096]{1,0:T(8,128)(2,1)S(1)} collective-permute-done((bf16[64,4096]{1,0:T(8,128)(2,1)S(1)}, bf16[64,4096]{1,0:T(8,128)(2,1)S(1)}, u32[]{:S(2)}, u32[]{:S(2)}) %collective-permute-start.1) | collective-permute-done | bytes 524320 | tf_op jit(solution)/shard_map/ppermute | solution.py:10
  229.2 5.0 all-to-all-start.6
  234.2 5.5 %fusion.2 = f32[192,768]{1,0:T(8,128)} fusion(bf16[192,4096]{1,0:T(8,128)(2,1)} %bitcast.31, bf16[1,1,4096,768]{3,2,1,0:T(8,128)(2,1)} %param.13), kind=kOutput, calls=%fused_computation.5 | convolution fusion | flops 1207959552 | bytes 8454144 | tf_op jit(solution)/shard_map/dot_general | solution.py:14
  239.7 15.4 %all-to-all-done.6 = bf16[8,24,4096]{2,1,0:T(8,128)(2,1)} async-done(((bf16[8,24,4096]{2,1,0:T(8,128)(2,1)}), bf16[8,24,4096]{2,1,0:T(8,128)(2,1)}, u32[]{:S(2)}, u32[]{:S(2)}) %all-to-all-start.6) | async-done | bytes 1572896 | tf_op jit(solution)/shard_map/all_to_all | solution.py:107
  255.0 4.7 fusion.24
  259.8 4.9 multiply_convert_fusion
  264.7 21.0 %convolution_convert_fusion = bf16[4096,1536]{0,1:T(8,128)(2,1)} fusion(bf16[192,4096]{1,0:T(8,128)(2,1)} %bitcast.31, bf16[192,4096]{1,0:T(8,128)(2,1)} %bitcast.20, bf16[192,4096]{1,0:T(8,128)(2,1)} %bitcast.8, bf16[192,768]{1,0:T(8,128)(2,1)S(1)} %get-tuple-element.20, bf16[192,768]{1,0:T(8,128)(2,1)S(1)} %get-tuple-element.17, ...), kind=kOutput, calls=%fused_computation.1 | convolution fusion | flops 7278821376 | bytes 19070976 | tf_op jit(solution)/shard_map/rc,rf->cf/dot_general | solution.py:147
  285.7 6.9 %convolution_convert_fusion.1 = bf16[4096,768]{0,1:T(8,128)(2,1)S(1)} fusion(bf16[192,4096]{1,0:T(8,128)(2,1)} %bitcast.28, bf16[192,4096]{1,0:T(8,128)(2,1)} %bitcast.17, bf16[192,4096]{1,0:T(8,128)(2,1)S(1)} %bitcast.167, bf16[192,768]{1,0:T(8,128)(2,1)S(1)} %get-tuple-element.18, bf16[192,768]{1,0:T(8,128)(2,1)S(1)} %copy-done.17, ...), kind=kOutput, calls=%fused_computation.2 | convolution fusion | flops 3643834368 | bytes 11894784 | tf_op jit(solution)/shard_map/rc,rf->cf/dot_general | solution.py:152
  292.6 16.4 %pad_maximum_fusion = bf16[4096,2304]{0,1:T(8,128)(2,1)} fusion(bf16[4096,768]{0,1:T(8,128)(2,1)S(1)} %convolution_convert_fusion.1, bf16[4096,1536]{0,1:T(8,128)(2,1)S(1)} %copy-done.2), kind=kLoop, calls=%fused_computation | loop fusion | flops 37748736 | bytes 37748736 | tf_op jit(solution)/shard_map/concatenate | solution.py:157
  309.0 5.0 fusion
  314.0 6.2 %fusion.39 = bf16[192,4096]{1,0:T(8,128)(2,1)} fusion(f32[192,4096]{1,0:T(8,128)S(1)} %fusion, bf16[192,768]{1,0:T(8,128)(2,1)S(1)} %get-tuple-element.20, bf16[1,1,4096,768]{3,2,1,0:T(8,128)(2,1)} %param.14), kind=kOutput, calls=%fused_computation.39 | convolution fusion | flops 1209532416 | bytes 11304960 | tf_op jit(solution)/shard_map/rf,df->rd/dot_general | solution.py:26
  320.1 5.2 all-to-all-start.8
  325.4 20.8 %all-to-all-done.8 = bf16[8,24,4096]{2,1,0:T(8,128)(2,1)} async-done(((bf16[8,24,4096]{2,1,0:T(8,128)(2,1)}), bf16[8,24,4096]{2,1,0:T(8,128)(2,1)}, u32[]{:S(2)}, u32[]{:S(2)}) %all-to-all-start.8) | async-done | bytes 1572896 | tf_op jit(solution)/shard_map/all_to_all | solution.py:124
  348.4 168.3 %reduce-scatter.2.cloned.1.call-done = bf16[512,2304]{0,1:T(8,128)(2,1)} async-done(((bf16[4096,2304]{0,1:T(8,128)(2,1)}), bf16[512,2304]{0,1:T(8,128)(2,1)}) %reduce-scatter.2.cloned.1.call-update) | async-done | bytes 2359312 | tf_op jit(solution)/shard_map/reduce_scatter | solution.py:156
  (114 shorter events, 50.5 us)
Async XLA Ops:
  7.2 13.4 %copy-start = (bf16[1,2,64,4096]{3,2,1,0:T(8,128)(2,1)S(1)}, bf16[1,2,64,4096]{3,2,1,0:T(8,128)(2,1)}, u32[]{:S(2)}) copy-start(bf16[1,2,64,4096]{3,2,1,0:T(8,128)(2,1)} %param.8) | copy-start | bytes 3145732
  13.8 27.5 %all-to-all-start = ((bf16[8,24,4096]{2,1,0:T(8,128)(2,1)}), bf16[8,24,4096]{2,1,0:T(8,128)(2,1)S(1)}, u32[]{:S(2)}, u32[]{:S(2)}) async-start(bf16[8,24,4096]{2,1,0:T(8,128)(2,1)} %bitcast.171), calls=%async_computation | async-start | bytes 3145728 | tf_op jit(solution)/shard_map/all_to_all | solution.py:107
  41.3 10.0 %copy-start.3 = (bf16[8,24,4096]{2,1,0:T(8,128)(2,1)}, bf16[8,24,4096]{2,1,0:T(8,128)(2,1)S(1)}, u32[]{:S(2)}) copy-start(bf16[8,24,4096]{2,1,0:T(8,128)(2,1)S(1)} %all-to-all-done) | copy-start | bytes 4718596
  41.3 25.9 %all-to-all-start.1 = ((bf16[8,24,4096]{2,1,0:T(8,128)(2,1)}), bf16[8,24,4096]{2,1,0:T(8,128)(2,1)}, u32[]{:S(2)}, u32[]{:S(2)}) async-start(bf16[8,24,4096]{2,1,0:T(8,128)(2,1)} %bitcast.7), calls=%async_computation.1 | async-start | bytes 3145728 | tf_op jit(solution)/shard_map/all_to_all | solution.py:100
  67.2 10.5 %slice-start = ((s8[6291456]{0:T(1024)(128)(4,1)}), s8[4194304]{0:T(1024)(128)(4,1)S(1)}, s32[]{:S(2)}) async-start(s8[6291456]{0:T(1024)(128)(4,1)} %bitcast.154), calls=%async_computation.11 | async-start | bytes 8388608
  67.2 12.7 %slice-start.4 = ((s8[6291456]{0:T(1024)(128)(4,1)}), s8[4194304]{0:T(1024)(128)(4,1)S(1)}, s32[]{:S(2)}) async-start(s8[6291456]{0:T(1024)(128)(4,1)} %bitcast.158), calls=%async_computation.15 | async-start | bytes 8388608
  72.0 5.7 %slice-start.1 = ((s8[6291456]{0:T(1024)(128)(4,1)}), s8[2097152]{0:T(1024)(128)(4,1)S(1)}, s32[]{:S(2)}) async-start(s8[6291456]{0:T(1024)(128)(4,1)} %bitcast.154), calls=%async_computation.12 | async-start | bytes 4194304
  72.0 7.9 %slice-start.5 = ((s8[6291456]{0:T(1024)(128)(4,1)}), s8[2097152]{0:T(1024)(128)(4,1)S(1)}, s32[]{:S(2)}) async-start(s8[6291456]{0:T(1024)(128)(4,1)} %bitcast.158), calls=%async_computation.16 | async-start | bytes 4194304
  83.3 25.1 %all-to-all-start.2 = ((bf16[8,24,4096]{2,1,0:T(8,128)(2,1)}), bf16[8,24,4096]{2,1,0:T(8,128)(2,1)S(1)}, u32[]{:S(2)}, u32[]{:S(2)}) async-start(bf16[8,24,4096]{2,1,0:T(8,128)(2,1)} %bitcast.11), calls=%async_computation.2 | async-start | bytes 3145728 | tf_op jit(solution)/shard_map/all_to_all | solution.py:124
  108.4 5.0 copy-start.5
  108.4 26.3 %all-to-all-start.4 = ((bf16[8,24,4096]{2,1,0:T(8,128)(2,1)}), bf16[8,24,4096]{2,1,0:T(8,128)(2,1)}, u32[]{:S(2)}, u32[]{:S(2)}) async-start(bf16[8,24,4096]{2,1,0:T(8,128)(2,1)} %bitcast.19), calls=%async_computation.4 | async-start | bytes 3145728 | tf_op jit(solution)/shard_map/all_to_all | solution.py:100
  116.3 15.6 %collective-permute-start = (bf16[64,4096]{1,0:T(8,128)(2,1)}, bf16[64,4096]{1,0:T(8,128)(2,1)S(1)}, u32[]{:S(2)}, u32[]{:S(2)}) collective-permute-start(bf16[64,4096]{1,0:T(8,128)(2,1)} %get-tuple-element.28), channel_id=1, source_target_pairs={{64,0},{65,1},{66,2},{67,3},{68,4},{69,5},{70,6},{71,7},{72,8},{73... | collective-permute-start | bytes 1572872 | tf_op jit(solution)/shard_map/ppermute | solution.py:10
  134.7 26.6 %all-to-all-start.3 = ((bf16[8,24,4096]{2,1,0:T(8,128)(2,1)}), bf16[8,24,4096]{2,1,0:T(8,128)(2,1)}, u32[]{:S(2)}, u32[]{:S(2)}) async-start(bf16[8,24,4096]{2,1,0:T(8,128)(2,1)} %bitcast.170), calls=%async_computation.3 | async-start | bytes 3145728 | tf_op jit(solution)/shard_map/all_to_all | solution.py:107
  161.3 10.5 %slice-start.2 = ((s8[6291456]{0:T(1024)(128)(4,1)}), s8[4194304]{0:T(1024)(128)(4,1)S(1)}, s32[]{:S(2)}) async-start(s8[6291456]{0:T(1024)(128)(4,1)} %bitcast.156), calls=%async_computation.13 | async-start | bytes 8388608
  161.3 12.7 %slice-start.6 = ((s8[6291456]{0:T(1024)(128)(4,1)}), s8[4194304]{0:T(1024)(128)(4,1)S(1)}, s32[]{:S(2)}) async-start(s8[6291456]{0:T(1024)(128)(4,1)} %bitcast.160), calls=%async_computation.17 | async-start | bytes 8388608
  166.1 5.7 %slice-start.3 = ((s8[6291456]{0:T(1024)(128)(4,1)}), s8[2097152]{0:T(1024)(128)(4,1)S(1)}, s32[]{:S(2)}) async-start(s8[6291456]{0:T(1024)(128)(4,1)} %bitcast.156), calls=%async_computation.14 | async-start | bytes 4194304
  166.1 7.9 %slice-start.7 = ((s8[6291456]{0:T(1024)(128)(4,1)}), s8[2097152]{0:T(1024)(128)(4,1)S(1)}, s32[]{:S(2)}) async-start(s8[6291456]{0:T(1024)(128)(4,1)} %bitcast.160), calls=%async_computation.18 | async-start | bytes 4194304
  177.4 25.9 %all-to-all-start.5 = ((bf16[8,24,4096]{2,1,0:T(8,128)(2,1)}), bf16[8,24,4096]{2,1,0:T(8,128)(2,1)}, u32[]{:S(2)}, u32[]{:S(2)}) async-start(bf16[8,24,4096]{2,1,0:T(8,128)(2,1)} %bitcast.21), calls=%async_computation.5 | async-start | bytes 3145728 | tf_op jit(solution)/shard_map/all_to_all | solution.py:124
  203.3 25.9 %all-to-all-start.7 = ((bf16[8,24,4096]{2,1,0:T(8,128)(2,1)}), bf16[8,24,4096]{2,1,0:T(8,128)(2,1)}, u32[]{:S(2)}, u32[]{:S(2)}) async-start(bf16[8,24,4096]{2,1,0:T(8,128)(2,1)} %bitcast.164), calls=%async_computation.7 | async-start | bytes 3145728 | tf_op jit(solution)/shard_map/all_to_all | solution.py:100
  210.4 15.3 %collective-permute-start.1 = (bf16[64,4096]{1,0:T(8,128)(2,1)S(1)}, bf16[64,4096]{1,0:T(8,128)(2,1)S(1)}, u32[]{:S(2)}, u32[]{:S(2)}) collective-permute-start(bf16[64,4096]{1,0:T(8,128)(2,1)S(1)} %get-tuple-element.8), channel_id=1, source_target_pairs={{64,0},{65,1},{66,2},{67,3},{68,4},{69,5},{70,6},{71,7},{72,8},{73... | collective-permute-start | bytes 1572872 | tf_op jit(solution)/shard_map/ppermute | solution.py:10
  225.7 14.0 %copy-start.12 = (bf16[64,4096]{1,0:T(8,128)(2,1)}, bf16[64,4096]{1,0:T(8,128)(2,1)S(1)}, u32[]{:S(2)}) copy-start(bf16[64,4096]{1,0:T(8,128)(2,1)S(1)} %collective-permute-done.1) | copy-start | bytes 1572868
  229.2 25.9 %all-to-all-start.6 = ((bf16[8,24,4096]{2,1,0:T(8,128)(2,1)}), bf16[8,24,4096]{2,1,0:T(8,128)(2,1)}, u32[]{:S(2)}, u32[]{:S(2)}) async-start(bf16[8,24,4096]{2,1,0:T(8,128)(2,1)} %bitcast.169), calls=%async_computation.6 | async-start | bytes 3145728 | tf_op jit(solution)/shard_map/all_to_all | solution.py:107
  234.2 282.5 %reduce-scatter.2.cloned.1.call-start = ((), (), s32[]{:S(2)}) async-start(), calls=%async_computation.10 | async-start | bytes 21233664 | tf_op jit(solution)/shard_map/reduce_scatter | solution.py:156
  259.8 4.9 copy-start.8
  259.8 4.9 copy-start.10
  264.7 21.0 %copy-start.4 = (bf16[8,24,4096]{2,1,0:T(8,128)(2,1)S(1)}, bf16[8,24,4096]{2,1,0:T(8,128)(2,1)}, u32[]{:S(2)}) copy-start(bf16[8,24,4096]{2,1,0:T(8,128)(2,1)} %copy-done.3) | copy-start | bytes 4718596
  264.7 21.0 %copy-start.16 = (bf16[192,768]{1,0:T(8,128)(2,1)S(1)}, bf16[192,768]{1,0:T(8,128)(2,1)}, u32[]{:S(2)}) copy-start(bf16[192,768]{1,0:T(8,128)(2,1)} %get-tuple-element.12) | copy-start | bytes 884740
  264.7 21.0 %copy-start.17 = (bf16[192,768]{1,0:T(8,128)(2,1)S(1)}, bf16[192,768]{1,0:T(8,128)(2,1)}, u32[]{:S(2)}) copy-start(bf16[192,768]{1,0:T(8,128)(2,1)} %get-tuple-element.15) | copy-start | bytes 884740
  285.7 6.9 %copy-start.2 = (bf16[4096,1536]{0,1:T(8,128)(2,1)S(1)}, bf16[4096,1536]{0,1:T(8,128)(2,1)}, u32[]{:S(2)}) copy-start(bf16[4096,1536]{0,1:T(8,128)(2,1)} %convolution_convert_fusion) | copy-start | bytes 37748740
  320.1 26.0 %copy-start.11 = (bf16[2,64,4096]{2,1,0:T(8,128)(2,1)S(1)}, bf16[2,64,4096]{2,1,0:T(8,128)(2,1)}, u32[]{:S(2)}) copy-start(bf16[2,64,4096]{2,1,0:T(8,128)(2,1)} %param.9) | copy-start | bytes 3145732
  320.1 26.0 %all-to-all-start.8 = ((bf16[8,24,4096]{2,1,0:T(8,128)(2,1)}), bf16[8,24,4096]{2,1,0:T(8,128)(2,1)}, u32[]{:S(2)}, u32[]{:S(2)}) async-start(bf16[8,24,4096]{2,1,0:T(8,128)(2,1)} %bitcast.32), calls=%async_computation.8 | async-start | bytes 3145728 | tf_op jit(solution)/shard_map/all_to_all | solution.py:124
  348.4 168.3 %copy-start.6 = (bf16[1,2,64,4096]{3,2,1,0:T(8,128)(2,1)}, bf16[1,2,64,4096]{3,2,1,0:T(8,128)(2,1)S(1)}, u32[]{:S(2)}) copy-start(bf16[1,2,64,4096]{3,2,1,0:T(8,128)(2,1)S(1)} %fusion.84) | copy-start | bytes 3145732
  (6 other events, 23.1 us)
Sparse Core Ops, SparseCore 0:
  309.1 207.5 reduce-scatter.1
where the time goes:
time: 537 us; the launch traced here: 528 us
  waiting for transfers between devices  319 us (59%)
  matrix products  118 us (22%)
  starting transfers between devices  49.9 us (9%)
  other arithmetic  19 us (4%)
  between operations  14.8 us (3%)
  local copies, waits for them, and re-layouts  7.58 us (1%)
    reduce_scatter x1, waiting for transfers between devices, local(): lax.psum_scatter(jnp.concatenate(pieces, axis=1).astype(jnp.bfloat16), 'd...  168 us
    all_to_all x3, waiting for transfers between devices, local(): lax.all_to_all(results, 'expert', split_axis=0, concat_axis=0, tiled=True)  56.9 us
    all_to_all x3, waiting for transfers between devices, local(): lax.all_to_all(scaled, 'expert', split_axis=0, concat_axis=0, tiled=True)  49.6 us
    ppermute x2, waiting for transfers between devices, shifted(): return lax.ppermute(value, axis, pairs)  27.5 us
    dot_general x1, matrix products, local(): jnp.einsum('rc,rf->cf', in_cols, all_gate_up[local_slot], preferred_eleme...  21 us
    all_to_all x3, starting transfers between devices, local(): lax.all_to_all(scaled, 'expert', split_axis=0, concat_axis=0, tiled=True)  17.7 us
    concatenate x1, other arithmetic, local(): jnp.concatenate(pieces, axis=1).astype(jnp.bfloat16)  16.4 us
    all_to_all x3, waiting for transfers between devices, local(): lax.all_to_all(picked.reshape(expert_size, block_rows, width), 'expert',...  16.3 us
  transfers between devices with their start and end apart: 12, of which 11 were waited for; matrix products, arithmetic and copies ran while one was open for 9% of the time, Pallas kernels for 0%

commit v1 on v0

v1 whole, which is shorter than its diff:
```python
import functools

import jax
import jax.numpy as jnp
from jax import lax
from jax.experimental import pallas as pl
from jax.experimental.pallas import tpu as pltpu
from jax.sharding import PartitionSpec as P

CAP = 24
NX = 4
F32 = jnp.float32
BF16 = jnp.bfloat16


def nt(left, right):
    return lax.dot_general(left, right, (((1,), (1,)), ((), ())), preferred_element_type=F32)


def nn(left, right):
    return jnp.dot(left, right, preferred_element_type=F32)


def mega(
    x_ref, cot_ref, posr_ref, posc_ref, rw_ref, wg_hbm, wu_hbm, wd_hbm,
    ig_ref, og_ref, ou_ref, od_ref,
    wg, wu, wd, xs, gs, xr, dr, ret, up, xsl, dsl, hh, aa, uu, yrecv,
    sel, selt, scale, a_acc, u_acc, q_acc,
    wsem, xss, xrs, gss, grs, dss, drs, lsem, pss, prs,
    xa_s, xa_r, da_s, da_r, h_s, h_r, ag_s, ag_r, au_s, au_r, ys, yr,
):
    p = lax.axis_index("pipe")
    me = lax.axis_index("expert")
    j = lax.axis_index("dp")
    ne = lax.axis_size("expert")
    ndp = lax.axis_size("dp")
    ny = ndp // NX
    x = lax.rem(j, NX)
    yh = j // NX
    last = lax.axis_size("pipe") - 1
    tokens, d = x_ref.shape
    rows = sel.shape[0]
    blk = rows // ne
    ff = wg.shape[2]
    cw = d // NX
    cp = cw // ny
    is_last = p == last

    def at_z(e):
        return (p, e, j)

    def at_x(k):
        return (p, me, yh * NX + k)

    def mesh_copy(src, dst, s, r, dev):
        return pltpu.make_async_remote_copy(
            src_ref=src, dst_ref=dst, send_sem=s, recv_sem=r,
            device_id=dev, device_id_type=pl.DeviceIdType.MESH,
        )

    y_peer = (p, me, lax.rem(yh + 1, ny) * NX + x)
    p_peer = (last - p, me, j)

    def w_copies(t, k):
        src, dst = ((wg_hbm, wg), (wu_hbm, wu), (wd_hbm, wd))[t]
        return [
            pltpu.make_async_copy(
                src.at[pl.ds(h * (d // ny) + k * cp, cp)],
                dst.at[k, pl.ds(h * cp, cp)],
                wsem.at[t, k, h],
            )
            for h in range(ny)
        ]

    for t in range(3):
        for k in range(NX):
            for c in w_copies(t, k):
                c.start()

    barrier = pltpu.get_barrier_semaphore()
    peers = [at_z(lax.rem(me + o, ne)) for o in range(1, ne)]
    peers += [at_x(lax.rem(x + o, NX)) for o in range(1, NX)]
    peers += [y_peer, p_peer]
    for dev in peers:
        pl.semaphore_signal(barrier, inc=1, device_id=dev, device_id_type=pl.DeviceIdType.MESH)

    r_iota = lax.broadcasted_iota(jnp.int32, (rows, tokens), 0)
    hit0 = r_iota == posr_ref[0:1, :]
    hit1 = r_iota == posr_ref[1:2, :]
    sel[...] = jnp.where(hit0 | hit1, 1.0, 0.0).astype(BF16)
    weight = jnp.where(hit0, rw_ref[0:1, :], 0.0) + jnp.where(hit1, rw_ref[1:2, :], 0.0)
    scale[...] = jnp.broadcast_to(jnp.sum(weight, axis=1, keepdims=True), scale.shape)
    c_iota = lax.broadcasted_iota(jnp.int32, (tokens, rows), 1)
    selt[...] = jnp.where(
        (c_iota == posc_ref[:, 0:1]) | (c_iota == posc_ref[:, 1:2]), 1.0, 0.0
    ).astype(BF16)

    pl.semaphore_wait(barrier, len(peers))

    def my_rows(e):
        return pl.ds(pl.multiple_of(e * blk, 16), blk)

    def z_sends(stage, land, ss, rs, k):
        out = []
        for o in range(1, ne):
            e = lax.rem(me + o, ne)
            out.append(
                mesh_copy(
                    stage.at[k, my_rows(e)], land.at[k, my_rows(me)],
                    ss.at[k, o], rs.at[k, o], at_z(e),
                )
            )
        return out

    def z_own(stage, land, ss, k):
        return pltpu.make_async_copy(
            stage.at[k, my_rows(me)], land.at[k, my_rows(me)], ss.at[k, 0]
        )

    def z_start(stage, land, ss, rs, k):
        for c in z_sends(stage, land, ss, rs, k):
            c.start()
        z_own(stage, land, ss, k).start()

    def z_recv(stage, land, ss, rs, k):
        for o in range(1, ne):
            e = lax.rem(me + ne - o, ne)
            mesh_copy(
                stage.at[k, my_rows(e)], land.at[k, my_rows(e)],
                ss.at[k, o], rs.at[k, o], at_z(e),
            ).wait_recv()
        z_own(stage, land, ss, k).wait()

    def z_done(stage, land, ss, rs, k):
        for c in z_sends(stage, land, ss, rs, k):
            c.wait_send()

    def piece(k, h):
        return pl.ds(pl.multiple_of(h * (d // ny) + k * cp, cp), cp)

    def chunk_of(ref, k):
        return jnp.concatenate([ref[:, piece(k, h)] for h in range(ny)], axis=1)

    def send_scaled(k):
        picked = nn(sel[...], up[k])
        gs[k] = (scale[:, 0:1] * picked).astype(BF16)
        z_start(gs, dr, gss, grs, k)

    @pl.loop(0, NX)
    def _(k):
        xs[k] = nn(sel[...], chunk_of(x_ref, k)).astype(BF16)
        z_start(xs, xr, xss, xrs, k)

        @pl.when(is_last)
        def _():
            up[k] = chunk_of(cot_ref, k)
            send_scaled(k)

    def share_copy(src, dst, ss, rs, k):
        return mesh_copy(src.at[k], dst.at[x], ss.at[k], rs.at[x], at_x(k))

    def share_local(src, dst, k, n):
        return pltpu.make_async_copy(src.at[k], dst.at[k], lsem.at[n])

    def share_start(src, dst, ss, rs, k, n):
        @pl.when(k != x)
        def _():
            share_copy(src, dst, ss, rs, k).start()

        @pl.when(k == x)
        def _():
            share_local(src, dst, k, n).start()

    def share_wait(src, dst, ss, rs, n):
        for o in range(1, NX):
            k = lax.rem(x + o, NX)
            share_copy(src, dst, ss, rs, k).wait_send()
            mesh_copy(src.at[k], dst.at[k], ss.at[k], rs.at[k], at_x(k)).wait_recv()
        share_local(src, dst, x, n).wait()

    def rows_of(s):
        return pl.ds(pl.multiple_of(s * rows, 16), rows)

    def gather(buf, ss, rs):
        return [
            mesh_copy(
                buf.at[rows_of(x)], buf.at[rows_of(x)], ss.at[o], rs.at[o],
                at_x(lax.rem(x + o, NX)),
            )
            for o in range(1, NX)
        ]

    def gather_start(buf, ss, rs):
        for c in gather(buf, ss, rs):
            c.start()

    def gather_wait(buf, ss, rs):
        for o, c in zip(range(1, NX), gather(buf, ss, rs)):
            c.wait_send()
            s = lax.rem(x + NX - o, NX)
            mesh_copy(
                buf.at[rows_of(s)], buf.at[rows_of(s)], ss.at[o], rs.at[o], at_x(s)
            ).wait_recv()

    tile = 256 if ff % 256 == 0 else ff

    a_acc[...] = jnp.zeros_like(a_acc)
    u_acc[...] = jnp.zeros_like(u_acc)
    q_acc[...] = jnp.zeros_like(q_acc)

    def wait_w(t, k):
        for c in w_copies(t, k):
            c.wait()

    @pl.loop(0, NX)
    def _(k):
        z_recv(xs, xr, xss, xrs, k)
        share_start(xr, xsl, xa_s, xa_r, k, 0)
        wait_w(0, k)
        wait_w(1, k)

        @pl.loop(0, ff // tile)
        def _(n):
            c = pl.ds(pl.multiple_of(n * tile, tile), tile)
            a_acc[:, c] += nn(xr[k], wg[k, :, c])
            u_acc[:, c] += nn(xr[k], wu[k, :, c])

    a = a_acc[...]
    hh[rows_of(x), :] = (a * jax.nn.sigmoid(a) * u_acc[...]).astype(BF16)
    gather_start(hh, h_s, h_r)

    def pipe_copy(k):
        return mesh_copy(up.at[k], up.at[k], pss.at[k], prs.at[k], p_peer)

    def take_dr(k):
        z_recv(gs, dr, gss, grs, k)
        share_start(dr, dsl, da_s, da_r, k, 1)
        wait_w(2, k)

        @pl.loop(0, ff // tile)
        def _(n):
            c = pl.ds(pl.multiple_of(n * tile, tile), tile)
            q_acc[:, c] += nn(dr[k], wd[k, :, c])

    @pl.loop(0, NX + 1)
    def _(k):
        @pl.when(jnp.logical_not(is_last) & (k < NX))
        def _():
            pipe_copy(k).wait_recv()
            send_scaled(k)

        @pl.when(k > 0)
        def _():
            take_dr(k - 1)

    a = a_acc[...]
    sg = jax.nn.sigmoid(a)
    q = q_acc[...]
    aa[rows_of(x), :] = (q * u_acc[...] * sg * (1.0 + a * (1.0 - sg))).astype(BF16)
    uu[rows_of(x), :] = (q * (a * sg)).astype(BF16)
    gather_start(aa, ag_s, ag_r)
    gather_start(uu, au_s, au_r)

    ct = 256 if cw % 256 == 0 else cw

    @pl.loop(0, NX)
    def _(k):
        z_done(xs, xr, xss, xrs, k)
        ga = aa[rows_of(x), :]
        gu = uu[rows_of(x), :]

        @pl.loop(0, cw // ct)
        def _(n):
            c = pl.ds(pl.multiple_of(n * ct, ct), ct)
            xs[k, :, c] = (nt(ga, wg[k, c, :]) + nt(gu, wu[k, c, :])).astype(BF16)

        z_start(xs, ret, dss, drs, k)

    @pl.loop(0, NX)
    def _(k):
        z_recv(xs, ret, dss, drs, k)
        total = (up[k].astype(F32) + nn(selt[...], ret[k])).astype(BF16)
        for h in range(ny):
            ig_ref[:, piece(k, h)] = total[:, h * cp : (h + 1) * cp]

        @pl.when(is_last)
        def _():
            up[k] = total
            pipe_copy(k).start()

    kh = wg.shape[2] // rows if wg.shape[2] % rows == 0 else 1

    def transposed(src, dst):
        for s in range(NX):
            for h in range(ny):
                dst[s // kh, h * cp : (h + 1) * cp, (s % kh) * rows : (s % kh + 1) * rows] = (
                    jnp.transpose(src[s, :, h * cp : (h + 1) * cp])
                )

    def product(lhs, rhs, h, n):
        c = pl.ds(pl.multiple_of(n * tile, tile), tile)
        r = pl.ds(pl.multiple_of(h * cp, cp), cp)
        acc = nn(lhs[0, r, :], rhs[0 : kh * rows, c])
        for m in range(1, NX // kh):
            acc += nn(lhs[m, r, :], rhs[m * kh * rows : (m + 1) * kh * rows, c])
        return acc

    def y_copy(t):
        return mesh_copy(wd.at[t, pl.ds(0, cp)], yrecv.at[t], ys.at[t], yr.at[t], y_peer)

    def for_peer(t, lhs, rhs):
        @pl.loop(0, ff // tile)
        def _(n):
            c = pl.ds(pl.multiple_of(n * tile, tile), tile)
            wd[t, 0:cp, c] = product(lhs, rhs, lax.rem(yh + 1, ny), n).astype(BF16)

        y_copy(t).start()

    def for_me(t, lhs, rhs, out):
        y_copy(t).wait()

        @pl.loop(0, ff // tile)
        def _(n):
            c = pl.ds(pl.multiple_of(n * tile, tile), tile)
            out[:, c] = (product(lhs, rhs, yh, n) + yrecv[t, :, c].astype(F32)).astype(BF16)

    share_wait(dr, dsl, da_s, da_r, 1)
    transposed(dsl, wu)
    gather_wait(hh, h_s, h_r)
    for_peer(0, wu, hh)
    share_wait(xr, xsl, xa_s, xa_r, 0)
    transposed(xsl, wg)
    gather_wait(aa, ag_s, ag_r)
    for_peer(1, wg, aa)
    gather_wait(uu, au_s, au_r)
    for_peer(2, wg, uu)
    for_me(0, wu, hh, od_ref)
    for_me(1, wg, aa, og_ref)
    for_me(2, wg, uu, ou_ref)

    @pl.loop(0, NX)
    def _(k):
        z_done(gs, dr, gss, grs, k)
        z_done(xs, ret, dss, drs, k)

        @pl.when(is_last)
        def _():
            pipe_copy(k).wait_send()


def slots_of(routes, placement):
    micro, count, top = routes.shape
    experts = placement.shape[0]
    match = routes.reshape(micro, count * top)[:, :, None] == placement
    slot = jnp.sum(jnp.where(match, jnp.arange(experts, dtype=jnp.int32), 0), axis=2)
    order = jnp.arange(count * top)
    before = order[None, :] < order[:, None]
    same = slot[:, :, None] == slot[:, None, :]
    rank = jnp.sum((same & before).astype(jnp.int32), axis=2)
    place = (slot * micro + jnp.arange(micro, dtype=jnp.int32)[:, None]) * CAP + rank
    return place.reshape(micro * count, top)


def local(
    activations, cotangent, routes, route_weights, placement, gate_weight, up_weight, down_weight
):
    ne = lax.axis_size("expert")
    ny = lax.axis_size("dp") // NX
    _, micro, count, d = activations.shape
    tokens = micro * count
    ff = gate_weight.shape[3]
    rows = ne * micro * CAP
    cw = d // NX
    cp = cw // ny
    place = slots_of(routes[0], placement[0])
    vm = functools.partial(pl.BlockSpec, memory_space=pltpu.VMEM)
    hbm = functools.partial(pl.BlockSpec, memory_space=pl.ANY)
    dma = pltpu.SemaphoreType.DMA
    wide = pltpu.VMEM((NX, rows, cw), BF16)
    tall = pltpu.VMEM((NX * rows, ff), BF16)
    weight = pltpu.VMEM((NX, cw, ff), BF16)
    acc = pltpu.VMEM((rows, ff), F32)
    outs = pl.pallas_call(
        mega,
        out_shape=(
            jax.ShapeDtypeStruct((tokens, d), BF16),
            jax.ShapeDtypeStruct((cp, ff), BF16),
            jax.ShapeDtypeStruct((cp, ff), BF16),
            jax.ShapeDtypeStruct((cp, ff), BF16),
        ),
        in_specs=[vm()] * 5 + [hbm()] * 3,
        out_specs=(vm(),) * 4,
        scratch_shapes=[
            weight, weight, weight,
            wide, wide, wide, wide, wide,
            pltpu.VMEM((NX, tokens, cw), BF16),
            wide, wide,
            tall, tall, tall,
            pltpu.VMEM((3, cp, ff), BF16),
            pltpu.VMEM((rows, tokens), BF16),
            pltpu.VMEM((tokens, rows), BF16),
            pltpu.VMEM((rows, 128), F32),
            acc, acc, acc,
            dma((3, NX, ny)),
            dma((NX, ne)), dma((NX, ne)), dma((NX, ne)), dma((NX, ne)),
            dma((NX, ne)), dma((NX, ne)),
            dma((2,)),
            dma((NX,)), dma((NX,)),
            dma((NX,)), dma((NX,)), dma((NX,)), dma((NX,)),
            dma((NX,)), dma((NX,)), dma((NX,)), dma((NX,)), dma((NX,)), dma((NX,)),
            dma((3,)), dma((3,)),
        ],
        compiler_params=pltpu.CompilerParams(
            collective_id=0, has_side_effects=True, vmem_limit_bytes=63 * 2**20
        ),
        cost_estimate=pl.CostEstimate(
            flops=20 * 10**9, bytes_accessed=24 * 10**6, transcendentals=10**6
        ),
    )(
        activations.reshape(tokens, d),
        cotangent.reshape(tokens, d),
        place.T,
        place,
        route_weights.reshape(tokens, -1).T,
        gate_weight[0, 0],
        up_weight[0, 0],
        down_weight[0, 0],
    )
    return (
        outs[0].reshape(1, micro, count, d),
        outs[1][None, None],
        outs[2][None, None],
        outs[3][None, None],
    )


def solution(mesh):
    blocks = ("expert", "dp")
    placed = (
        P("pipe", None, blocks, None),
        P(None, blocks, None),
        P("pipe", None, blocks, None),
        P("pipe", None, blocks, None),
        P("pipe", None),
        P("pipe", "expert", None, None),
        P("pipe", "expert", None, None),
        P("pipe", "expert", None, None),
    )
    return jax.shard_map(
        local,
        mesh=mesh,
        in_specs=placed,
        out_specs=(
            P("pipe", None, blocks, None),
            P("pipe", "expert", "dp", None),
            P("pipe", "expert", "dp", None),
            P("pipe", "expert", "dp", None),
        ),
        check_vma=False,
    )
```

time: 537 us -> 271 us (0.50); the launches traced: 528 us -> 271 us
  waiting for transfers between devices: 319 us -> 0 us
  Pallas kernels: 0 us -> 257 us
  matrix products: 118 us -> 0 us
  starting transfers between devices: 49.9 us -> 0 us
  other arithmetic: 19 us -> 1.02 us
  between operations: 14.8 us -> 0.7 us
    pallas_call x0 -> x1, Pallas kernels: none -> 257 us  [local(): pl.pallas_call(mega, out_shape=(jax.ShapeDtypeStruct((tokens, d), BF16),...]
    reduce_scatter x1 -> x0, waiting for transfers between devices: 168 us -> none  [local(): lax.psum_scatter(jnp.concatenate(pieces, axis=1).astype(jnp.bfloat16), 'd...]
    all_to_all x9 -> x0, waiting for transfers between devices: 123 us -> none  [the longest x3 56.9 us: local(): lax.all_to_all(results, 'expert', split_axis=0, concat_axis=0, tiled=True)]
    dot_general x29 -> x0, matrix products: 118 us -> none  [the longest x1 21 us: local(): jnp.einsum('rc,rf->cf', in_cols, all_gate_up[local_slot], preferred_eleme...]
    all_to_all x9 -> x0, starting transfers between devices: 47.4 us -> none  [the longest x3 17.7 us: local(): lax.all_to_all(scaled, 'expert', split_axis=0, concat_axis=0, tiled=True)]
    ppermute x2 -> x0, waiting for transfers between devices: 27.5 us -> none  [shifted(): return lax.ppermute(value, axis, pairs)]
    concatenate x1 -> x0, other arithmetic: 16.4 us -> none  [local(): jnp.concatenate(pieces, axis=1).astype(jnp.bfloat16)]
    unnamed x53 -> x8, local copies, waits for them, and re-layouts: 0.2 us -> 9.94 us
  transfers between devices with their start and end apart: 12 -> 0, of which waited for: 11 -> 0; matrix products, arithmetic and copies ran while one was open for 9% -> 0% of each run, Pallas kernels for 0% -> 0%
where the time goes in v1:
time: 271 us
  Pallas kernels  257 us (95%)
  local copies, waits for them, and re-layouts  11.7 us (4%)
    pallas_call x1, Pallas kernels, local(): pl.pallas_call(mega, out_shape=(jax.ShapeDtypeStruct((tokens, d), BF16),...  257 us
    unnamed x8, local copies, waits for them, and re-layouts  9.94 us

profile of v1, /device:TPU:1, one launch (start us, length us, event | category | flops | bytes accessed | tf_op | source)
XLA Modules:
  0.0 270.9 jit_solution(18251136048852593086)
XLA Ops:
  0.6 0.1 add.18
  0.7 0.7 copy.18
  1.4 0.6 reshape.44
  2.1 0.8 copy.17
  2.9 0.1 eq.30
  3.0 0.7 select_reduce_fusion
  3.7 0.2 convert_reduce_fusion
  3.9 0.1 mul.19
  4.1 0.1 reduce_sum.22
  4.2 0.1 multiply_add_fusion.posc_ref
  4.3 0.0 copy-start
  4.3 0.6 copy.19.posr_ref
  5.0 0.0 copy-done
  5.0 257.5 %shard_map.111 = (bf16[128,4096]{1,0:T(8,128)(2,1)}, bf16[512,768]{1,0:T(8,128)(2,1)}, bf16[512,768]{1,0:T(8,128)(2,1)}, bf16[512,768]{1,0:T(8,128)(2,1)}) custom-call(bf16[128,4096]{1,0:T(8,128)(2,1)} %bitcast.26, bf16[128,4096]{1,0:T(8,128)(2,1)} %bitcast.27, s32[2,128]{1,0:T(2,128)} %copy.19.posr_ref, s32[128,2]{1,0:T(8,128)} %copy-done, ...), custom_call_target="tpu_custom_call" | custom-call | flops 20000000000 | bytes 24000000 | tf_op jit(solution)/shard_map/pallas_call | solution.py:383
  262.5 2.3 copy.24
  264.8 2.1 copy.25
  266.8 2.1 copy.26
  268.9 2.1 copy.27
  (3 shorter events, 0.0 us)
Async XLA Ops:
  4.3 0.7 copy-start

commit v2 on v1

--- a/solution.py
+++ b/solution.py
@@ -27,7 +27,7 @@
     wg, wu, wd, xs, gs, xr, dr, ret, up, xsl, dsl, hh, aa, uu, yrecv,
     sel, selt, scale, a_acc, u_acc, q_acc,
     wsem, xss, xrs, gss, grs, dss, drs, lsem, pss, prs,
-    xa_s, xa_r, da_s, da_r, h_s, h_r, ag_s, ag_r, au_s, au_r, ys, yr,
+    xa_s, xa_r, da_s, da_r, h_s, h_r, ag_s, ag_r, au_s, au_r, ys, yr, igs, gos,
 ):
     p = lax.axis_index("pipe")
     me = lax.axis_index("expert")
@@ -146,8 +146,12 @@
         gs[k] = (scale[:, 0:1] * picked).astype(BF16)
         z_start(gs, dr, gss, grs, k)
 
+    def turn(step):
+        return lax.rem(x + step, NX)
+
     @pl.loop(0, NX)
-    def _(k):
+    def _(step):
+        k = turn(step)
         xs[k] = nn(sel[...], chunk_of(x_ref, k)).astype(BF16)
         z_start(xs, xr, xss, xrs, k)
 
@@ -213,7 +217,8 @@
             c.wait()
 
     @pl.loop(0, NX)
-    def _(k):
+    def _(step):
+        k = turn(step)
         z_recv(xs, xr, xss, xrs, k)
         share_start(xr, xsl, xa_s, xa_r, k, 0)
         wait_w(0, k)
@@ -243,15 +248,15 @@
             q_acc[:, c] += nn(dr[k], wd[k, :, c])
 
     @pl.loop(0, NX + 1)
-    def _(k):
-        @pl.when(jnp.logical_not(is_last) & (k < NX))
+    def _(step):
+        @pl.when(jnp.logical_not(is_last) & (step < NX))
         def _():
-            pipe_copy(k).wait_recv()
-            send_scaled(k)
-
-        @pl.when(k > 0)
+            pipe_copy(turn(step)).wait_recv()
+            send_scaled(turn(step))
+
+        @pl.when(step > 0)
         def _():
-            take_dr(k - 1)
+            take_dr(turn(step + NX - 1))
 
     a = a_acc[...]
     sg = jax.nn.sigmoid(a)
@@ -264,7 +269,8 @@
     ct = 256 if cw % 256 == 0 else cw
 
     @pl.loop(0, NX)
-    def _(k):
+    def _(step):
+        k = turn(step)
         z_done(xs, xr, xss, xrs, k)
         ga = aa[rows_of(x), :]
         gu = uu[rows_of(x), :]
@@ -276,17 +282,31 @@
 
         z_start(xs, ret, dss, drs, k)
 
-    @pl.loop(0, NX)
-    def _(k):
-        z_recv(xs, ret, dss, drs, k)
-        total = (up[k].astype(F32) + nn(selt[...], ret[k])).astype(BF16)
-        for h in range(ny):
-            ig_ref[:, piece(k, h)] = total[:, h * cp : (h + 1) * cp]
-
-        @pl.when(is_last)
-        def _():
-            up[k] = total
-            pipe_copy(k).start()
+    def ig_copies(k):
+        return [
+            pltpu.make_async_copy(
+                up.at[k, :, pl.ds(h * cp, cp)], ig_ref.at[:, piece(k, h)], igs.at[k, h]
+            )
+            for h in range(ny)
+        ]
+
+    def combine():
+        @pl.loop(0, NX)
+        def _(step):
+            k = turn(step)
+            z_recv(xs, ret, dss, drs, k)
+            up[k] = (up[k].astype(F32) + nn(selt[...], ret[k])).astype(BF16)
+
+            @pl.when(is_last)
+            def _():
+                pipe_copy(k).start()
+
+            for c in ig_copies(k):
+                c.start()
+
+    @pl.when(is_last)
+    def _():
+        combine()
 
     kh = wg.shape[2] // rows if wg.shape[2] % rows == 0 else 1
 
@@ -316,13 +336,21 @@
 
         y_copy(t).start()
 
-    def for_me(t, lhs, rhs, out):
+    def out_copy(t):
+        out = (od_ref, og_ref, ou_ref)[t]
+        return pltpu.make_async_copy(wd.at[t, pl.ds(cp, cp)], out, gos.at[t])
+
+    def for_me(t, lhs, rhs):
         y_copy(t).wait()
 
         @pl.loop(0, ff // tile)
         def _(n):
             c = pl.ds(pl.multiple_of(n * tile, tile), tile)
-            out[:, c] = (product(lhs, rhs, yh, n) + yrecv[t, :, c].astype(F32)).astype(BF16)
+            wd[t, cp : 2 * cp, c] = (
+                product(lhs, rhs, yh, n) + yrecv[t, :, c].astype(F32)
+            ).astype(BF16)
+
+        out_copy(t).start()
 
     share_wait(dr, dsl, da_s, da_r, 1)
     transposed(dsl, wu)
@@ -330,22 +358,47 @@
     for_peer(0, wu, hh)
     share_wait(xr, xsl, xa_s, xa_r, 0)
     transposed(xsl, wg)
+
+    @pl.when(jnp.logical_not(is_last))
+    def _():
+        combine()
+
     gather_wait(aa, ag_s, ag_r)
     for_peer(1, wg, aa)
     gather_wait(uu, au_s, au_r)
     for_peer(2, wg, uu)
-    for_me(0, wu, hh, od_ref)
-    for_me(1, wg, aa, og_ref)
-    for_me(2, wg, uu, ou_ref)
+    for_me(0, wu, hh)
+    for_me(1, wg, aa)
+    for_me(2, wg, uu)
 
     @pl.loop(0, NX)
     def _(k):
         z_done(gs, dr, gss, grs, k)
         z_done(xs, ret, dss, drs, k)
+        for c in ig_copies(k):
+            c.wait()
 
         @pl.when(is_last)
         def _():
             pipe_copy(k).wait_send()
+
+    for t in range(3):
+        out_copy(t).wait()
+
+
+def settle(*refs):
+    count = (len(refs) - 2) // 3
+    ins, outs, held = refs[:count], refs[count : 2 * count], refs[2 * count : 3 * count]
+    got, put = refs[-2:]
+    loads = [pltpu.make_async_copy(ins[i], held[i], got.at[i]) for i in range(count)]
+    stores = [pltpu.make_async_copy(held[i], outs[i], put.at[i]) for i in range(count)]
+    for c in loads:
+        c.start()
+    for load, store in zip(loads, stores):
+        load.wait()
+        store.start()
+    for c in stores:
+        c.wait()
 
 
 def slots_of(routes, placement):
@@ -389,7 +442,7 @@
             jax.ShapeDtypeStruct((cp, ff), BF16),
         ),
         in_specs=[vm()] * 5 + [hbm()] * 3,
-        out_specs=(vm(),) * 4,
+        out_specs=(hbm(),) * 4,
         scratch_shapes=[
             weight, weight, weight,
             wide, wide, wide, wide, wide,
@@ -408,7 +461,7 @@
             dma((NX,)), dma((NX,)),
             dma((NX,)), dma((NX,)), dma((NX,)), dma((NX,)),
             dma((NX,)), dma((NX,)), dma((NX,)), dma((NX,)), dma((NX,)), dma((NX,)),
-            dma((3,)), dma((3,)),
+            dma((3,)), dma((3,)), dma((NX, ny)), dma((3,)),
         ],
         compiler_params=pltpu.CompilerParams(
             collective_id=0, has_side_effects=True, vmem_limit_bytes=63 * 2**20
@@ -426,6 +479,13 @@
         up_weight[0, 0],
         down_weight[0, 0],
     )
+    outs = pl.pallas_call(
+        settle,
+        out_shape=tuple(jax.ShapeDtypeStruct(o.shape, o.dtype) for o in outs),
+        in_specs=[hbm()] * 4,
+        out_specs=(hbm(),) * 4,
+        scratch_shapes=[pltpu.VMEM(o.shape, o.dtype) for o in outs] + [dma((4,)), dma((4,))],
+    )(*outs)
     return (
         outs[0].reshape(1, micro, count, d),
         outs[1][None, None],

time: 271 us -> 248 us (0.915)
  Pallas kernels: 257 us -> 243 us
  local copies, waits for them, and re-layouts: 11.7 us -> 3.25 us
    pallas_call x1, Pallas kernels: 257 us -> 240 us  [local(): pl.pallas_call(mega, out_shape=(jax.ShapeDtypeStruct((tokens, d), BF16),...]
    unnamed x8 -> x4, local copies, waits for them, and re-layouts: 9.94 us -> 1.47 us
    pallas_call x0 -> x1, Pallas kernels: none -> 3.04 us  [local(): pl.pallas_call(settle, out_shape=tuple((jax.ShapeDtypeStruct(o.shape, o.d...]
where the time goes in v2:
time: 248 us
  Pallas kernels  243 us (98%)
  local copies, waits for them, and re-layouts  3.25 us (1%)
    pallas_call x1, Pallas kernels, local(): pl.pallas_call(mega, out_shape=(jax.ShapeDtypeStruct((tokens, d), BF16),...  240 us

profile of v2, /device:TPU:1, one launch (start us, length us, event | category | flops | bytes accessed | tf_op | source)
XLA Modules:
  0.0 248.0 jit_solution(14925137178975926234)
XLA Ops:
  0.6 0.1 add.18
  0.7 0.7 copy.18
  1.4 0.6 reshape.44
  2.1 0.8 copy.17
  2.9 0.1 eq.30
  3.0 0.7 select_reduce_fusion
  3.7 0.2 convert_reduce_fusion
  3.9 0.1 mul.19
  4.1 0.1 reduce_sum.22
  4.2 0.1 multiply_add_fusion.posc_ref
  4.3 0.0 copy-start
  4.3 0.6 copy.19.posr_ref
  5.0 0.0 copy-done
  5.0 240.0 %shard_map.111 = (bf16[128,4096]{1,0:T(8,128)(2,1)}, bf16[512,768]{1,0:T(8,128)(2,1)}, bf16[512,768]{1,0:T(8,128)(2,1)}, bf16[512,768]{1,0:T(8,128)(2,1)}) custom-call(bf16[128,4096]{1,0:T(8,128)(2,1)} %bitcast.22, bf16[128,4096]{1,0:T(8,128)(2,1)} %bitcast.23, s32[2,128]{1,0:T(2,128)} %copy.19.posr_ref, s32[128,2]{1,0:T(8,128)} %copy-done, ...), custom_call_target="tpu_custom_call" | custom-call | flops 20000000000 | bytes 24000000 | tf_op jit(solution)/shard_map/pallas_call | solution.py:436
  244.9 3.0 %shard_map.112 = (bf16[128,4096]{1,0:T(8,128)(2,1)}, bf16[512,768]{1,0:T(8,128)(2,1)}, bf16[512,768]{1,0:T(8,128)(2,1)}, bf16[512,768]{1,0:T(8,128)(2,1)}) custom-call(bf16[128,4096]{1,0:T(8,128)(2,1)} %get-tuple-element.12.refs_0_, bf16[512,768]{1,0:T(8,128)(2,1)} %get-tuple-element.13.refs_1_, bf16[512,768]{1,0:T(8,128)(2,1)} %get-tuple-element.14.refs_2_, ...), custom_call_target="tpu_custom_call" | custom-call | tf_op jit(solution)/shard_map/pallas_call | solution.py:482
  (3 shorter events, 0.0 us)
Async XLA Ops:
  4.3 0.7 copy-start

commit v3 on v2

--- a/solution.py
+++ b/solution.py
@@ -22,7 +22,7 @@
 
 
 def mega(
-    x_ref, cot_ref, posr_ref, posc_ref, rw_ref, wg_hbm, wu_hbm, wd_hbm,
+    micro, x_ref, cot_ref, routes_ref, rw_ref, place_ref, wg_hbm, wu_hbm, wd_hbm,
     ig_ref, og_ref, ou_ref, od_ref,
     wg, wu, wd, xs, gs, xr, dr, ret, up, xsl, dsl, hh, aa, uu, yrecv,
     sel, selt, scale, a_acc, u_acc, q_acc,
@@ -84,16 +84,39 @@
     for dev in peers:
         pl.semaphore_signal(barrier, inc=1, device_id=dev, device_id_type=pl.DeviceIdType.MESH)
 
-    r_iota = lax.broadcasted_iota(jnp.int32, (rows, tokens), 0)
-    hit0 = r_iota == posr_ref[0:1, :]
-    hit1 = r_iota == posr_ref[1:2, :]
-    sel[...] = jnp.where(hit0 | hit1, 1.0, 0.0).astype(BF16)
-    weight = jnp.where(hit0, rw_ref[0:1, :], 0.0) + jnp.where(hit1, rw_ref[1:2, :], 0.0)
+    square = (tokens, tokens)
+    t_row = lax.broadcasted_iota(jnp.int32, square, 0)
+    t_col = lax.broadcasted_iota(jnp.int32, square, 1)
+    count = tokens // micro
+    before = (t_col < t_row) & (t_col // count == t_row // count)
+    ids = routes_ref[...]
+    slots = jnp.zeros(ids.shape, jnp.int32)
+    for s in range(ne):
+        slots = jnp.where(ids == place_ref[0, s], s, slots)
+    slots = slots.astype(F32)
+    by_row = [jnp.broadcast_to(slots[:, k : k + 1], square) for k in range(2)]
+    by_col = [jnp.transpose(v) for v in by_row]
+    micro_of = (lax.broadcasted_iota(jnp.int32, (tokens, 1), 0) // count).astype(F32)
+    places = []
+    for k in range(2):
+        same = jnp.where(by_col[0] == by_row[k], 1.0, 0.0) + jnp.where(
+            by_col[1] == by_row[k], 1.0, 0.0
+        )
+        rank = jnp.sum(jnp.where(before, same, 0.0), axis=1, keepdims=True)
+        places.append(slots[:, k : k + 1] * blk + micro_of * CAP + rank)
+
+    def as_row(column):
+        return jnp.transpose(jnp.broadcast_to(column, square))[0:1, :]
+
+    r_iota = lax.broadcasted_iota(jnp.int32, (rows, tokens), 0).astype(F32)
+    hits = [r_iota == as_row(v) for v in places]
+    sel[...] = jnp.where(hits[0] | hits[1], 1.0, 0.0).astype(BF16)
+    weight = sum(
+        jnp.where(hits[k], as_row(rw_ref[:, k : k + 1]), 0.0) for k in range(2)
+    )
     scale[...] = jnp.broadcast_to(jnp.sum(weight, axis=1, keepdims=True), scale.shape)
-    c_iota = lax.broadcasted_iota(jnp.int32, (tokens, rows), 1)
-    selt[...] = jnp.where(
-        (c_iota == posc_ref[:, 0:1]) | (c_iota == posc_ref[:, 1:2]), 1.0, 0.0
-    ).astype(BF16)
+    c_iota = lax.broadcasted_iota(jnp.int32, (tokens, rows), 1).astype(F32)
+    selt[...] = jnp.where((c_iota == places[0]) | (c_iota == places[1]), 1.0, 0.0).astype(BF16)
 
     pl.semaphore_wait(barrier, len(peers))
 
@@ -206,7 +229,38 @@
                 buf.at[rows_of(s)], buf.at[rows_of(s)], ss.at[o], rs.at[o], at_x(s)
             ).wait_recv()
 
-    tile = 256 if ff % 256 == 0 else ff
+    tile = 256
+
+    pieces = ff // tile
+    half = rows // 2
+    right, left = lax.rem(x + 1, NX), lax.rem(x + NX - 1, NX)
+    across = lax.rem(x + 2, NX)
+
+    def ring_copy(buf, ss, rs, n, way, owner, first, count, to):
+        part = buf.at[
+            pl.ds(pl.multiple_of(owner * rows + first, 16), count), pl.ds(n * tile, tile)
+        ]
+        return mesh_copy(part, part, ss.at[n, way], rs.at[n, way], at_x(to))
+
+    def ring_start(buf, ss, rs, n):
+        ring_copy(buf, ss, rs, n, 0, x, 0, rows, right).start()
+        ring_copy(buf, ss, rs, n, 1, x, 0, rows, left).start()
+
+    def ring_pass(buf, ss, rs, n):
+        ring_copy(buf, ss, rs, n, 0, left, 0, rows, right).wait_recv()
+        ring_copy(buf, ss, rs, n, 2, left, 0, half, right).start()
+        ring_copy(buf, ss, rs, n, 1, right, 0, rows, left).wait_recv()
+        ring_copy(buf, ss, rs, n, 3, right, half, half, left).start()
+
+    def ring_wait(buf, ss, rs, n):
+        ring_copy(buf, ss, rs, n, 2, across, 0, half, right).wait_recv()
+        ring_copy(buf, ss, rs, n, 3, across, half, half, left).wait_recv()
+
+    def ring_done(buf, ss, rs, n):
+        ring_copy(buf, ss, rs, n, 0, x, 0, rows, right).wait_send()
+        ring_copy(buf, ss, rs, n, 1, x, 0, rows, left).wait_send()
+        ring_copy(buf, ss, rs, n, 2, left, 0, half, right).wait_send()
+        ring_copy(buf, ss, rs, n, 3, right, half, half, left).wait_send()
 
     a_acc[...] = jnp.zeros_like(a_acc)
     u_acc[...] = jnp.zeros_like(u_acc)
@@ -263,8 +317,10 @@
     q = q_acc[...]
     aa[rows_of(x), :] = (q * u_acc[...] * sg * (1.0 + a * (1.0 - sg))).astype(BF16)
     uu[rows_of(x), :] = (q * (a * sg)).astype(BF16)
-    gather_start(aa, ag_s, ag_r)
-    gather_start(uu, au_s, au_r)
+    for n in range(pieces):
+        ring_start(aa, ag_s, ag_r, n)
+    for n in range(pieces):
+        ring_start(uu, au_s, au_r, n)
 
     ct = 256 if cw % 256 == 0 else cw
 
@@ -317,59 +373,69 @@
                     jnp.transpose(src[s, :, h * cp : (h + 1) * cp])
                 )
 
+    def columns(n):
+        return pl.ds(n * tile, tile)
+
     def product(lhs, rhs, h, n):
-        c = pl.ds(pl.multiple_of(n * tile, tile), tile)
+        c = columns(n)
         r = pl.ds(pl.multiple_of(h * cp, cp), cp)
         acc = nn(lhs[0, r, :], rhs[0 : kh * rows, c])
         for m in range(1, NX // kh):
             acc += nn(lhs[m, r, :], rhs[m * kh * rows : (m + 1) * kh * rows, c])
         return acc
 
-    def y_copy(t):
-        return mesh_copy(wd.at[t, pl.ds(0, cp)], yrecv.at[t], ys.at[t], yr.at[t], y_peer)
-
-    def for_peer(t, lhs, rhs):
-        @pl.loop(0, ff // tile)
-        def _(n):
-            c = pl.ds(pl.multiple_of(n * tile, tile), tile)
-            wd[t, 0:cp, c] = product(lhs, rhs, lax.rem(yh + 1, ny), n).astype(BF16)
-
-        y_copy(t).start()
-
-    def out_copy(t):
+    def y_copy(t, n):
+        return mesh_copy(
+            wd.at[t, pl.ds(0, cp), columns(n)], yrecv.at[t, :, columns(n)],
+            ys.at[t, n], yr.at[t, n], y_peer,
+        )
+
+    def for_peer(t, lhs, rhs, n):
+        wd[t, 0:cp, columns(n)] = product(lhs, rhs, lax.rem(yh + 1, ny), n).astype(BF16)
+        y_copy(t, n).start()
+
+    def out_copy(t, n):
         out = (od_ref, og_ref, ou_ref)[t]
-        return pltpu.make_async_copy(wd.at[t, pl.ds(cp, cp)], out, gos.at[t])
-
-    def for_me(t, lhs, rhs):
-        y_copy(t).wait()
-
-        @pl.loop(0, ff // tile)
-        def _(n):
-            c = pl.ds(pl.multiple_of(n * tile, tile), tile)
-            wd[t, cp : 2 * cp, c] = (
-                product(lhs, rhs, yh, n) + yrecv[t, :, c].astype(F32)
-            ).astype(BF16)
-
-        out_copy(t).start()
-
+        return pltpu.make_async_copy(
+            wd.at[t, pl.ds(cp, cp), columns(n)], out.at[:, columns(n)], gos.at[t, n]
+        )
+
+    def for_me(t, lhs, rhs, n):
+        mine = product(lhs, rhs, yh, n)
+        y_copy(t, n).wait()
+        wd[t, cp : 2 * cp, columns(n)] = (
+            mine + yrecv[t, :, columns(n)].astype(F32)
+        ).astype(BF16)
+        out_copy(t, n).start()
+
+    ring = [(aa, ag_s, ag_r, n) for n in range(pieces)]
+    ring += [(uu, au_s, au_r, n) for n in range(pieces)]
+    ring_pass(*ring[0])
     share_wait(dr, dsl, da_s, da_r, 1)
     transposed(dsl, wu)
+    ring_pass(*ring[1])
     gather_wait(hh, h_s, h_r)
-    for_peer(0, wu, hh)
+    for n in range(pieces):
+        for_peer(0, wu, hh, n)
+    ring_pass(*ring[2])
     share_wait(xr, xsl, xa_s, xa_r, 0)
     transposed(xsl, wg)
+    for i in range(len(ring)):
+        if i + 3 < len(ring):
+            ring_pass(*ring[i + 3])
+        ring_wait(*ring[i])
+        for_peer(1 + i // pieces, wg, ring[i][0], i % pieces)
 
     @pl.when(jnp.logical_not(is_last))
     def _():
         combine()
 
-    gather_wait(aa, ag_s, ag_r)
-    for_peer(1, wg, aa)
-    gather_wait(uu, au_s, au_r)
-    for_peer(2, wg, uu)
-    for_me(0, wu, hh)
-    for_me(1, wg, aa)
-    for_me(2, wg, uu)
+    for n in range(pieces):
+        for_me(0, wu, hh, n)
+    for i in range(len(ring)):
+        for_me(1 + i // pieces, wg, ring[i][0], i % pieces)
+    for args in ring:
+        ring_done(*args)
 
     @pl.loop(0, NX)
     def _(k):
@@ -383,7 +449,8 @@
             pipe_copy(k).wait_send()
 
     for t in range(3):
-        out_copy(t).wait()
+        for n in range(pieces):
+            out_copy(t, n).wait()
 
 
 def settle(*refs):
@@ -401,19 +468,6 @@
         c.wait()
 
 
-def slots_of(routes, placement):
-    micro, count, top = routes.shape
-    experts = placement.shape[0]
-    match = routes.reshape(micro, count * top)[:, :, None] == placement
-    slot = jnp.sum(jnp.where(match, jnp.arange(experts, dtype=jnp.int32), 0), axis=2)
-    order = jnp.arange(count * top)
-    before = order[None, :] < order[:, None]
-    same = slot[:, :, None] == slot[:, None, :]
-    rank = jnp.sum((same & before).astype(jnp.int32), axis=2)
-    place = (slot * micro + jnp.arange(micro, dtype=jnp.int32)[:, None]) * CAP + rank
-    return place.reshape(micro * count, top)
-
-
 def local(
     activations, cotangent, routes, route_weights, placement, gate_weight, up_weight, down_weight
 ):
@@ -425,7 +479,6 @@
     rows = ne * micro * CAP
     cw = d // NX
     cp = cw // ny
-    place = slots_of(routes[0], placement[0])
     vm = functools.partial(pl.BlockSpec, memory_space=pltpu.VMEM)
     hbm = functools.partial(pl.BlockSpec, memory_space=pl.ANY)
     dma = pltpu.SemaphoreType.DMA
@@ -433,15 +486,16 @@
     tall = pltpu.VMEM((NX * rows, ff), BF16)
     weight = pltpu.VMEM((NX, cw, ff), BF16)
     acc = pltpu.VMEM((rows, ff), F32)
+    np_ = ff // 256
     outs = pl.pallas_call(
-        mega,
+        functools.partial(mega, micro),
         out_shape=(
             jax.ShapeDtypeStruct((tokens, d), BF16),
             jax.ShapeDtypeStruct((cp, ff), BF16),
             jax.ShapeDtypeStruct((cp, ff), BF16),
             jax.ShapeDtypeStruct((cp, ff), BF16),
         ),
-        in_specs=[vm()] * 5 + [hbm()] * 3,
+        in_specs=[vm()] * 4 + [pl.BlockSpec(memory_space=pltpu.SMEM)] + [hbm()] * 3,
         out_specs=(hbm(),) * 4,
         scratch_shapes=[
             weight, weight, weight,
@@ -460,8 +514,8 @@
             dma((2,)),
             dma((NX,)), dma((NX,)),
             dma((NX,)), dma((NX,)), dma((NX,)), dma((NX,)),
-            dma((NX,)), dma((NX,)), dma((NX,)), dma((NX,)), dma((NX,)), dma((NX,)),
-            dma((3,)), dma((3,)), dma((NX, ny)), dma((3,)),
+            dma((NX,)), dma((NX,)), dma((np_, 4)), dma((np_, 4)), dma((np_, 4)), dma((np_, 4)),
+            dma((3, np_)), dma((3, np_)), dma((NX, ny)), dma((3, np_)),
         ],
         compiler_params=pltpu.CompilerParams(
             collective_id=0, has_side_effects=True, vmem_limit_bytes=63 * 2**20
@@ -472,9 +526,9 @@
     )(
         activations.reshape(tokens, d),
         cotangent.reshape(tokens, d),
-        place.T,
-        place,
-        route_weights.reshape(tokens, -1).T,
+        routes.reshape(tokens, -1),
+        route_weights.reshape(tokens, -1),
+        placement,
         gate_weight[0, 0],
         up_weight[0, 0],
         down_weight[0, 0],

time: 248 us -> 238 us (0.960)
  Pallas kernels: 243 us -> 234 us
    pallas_call x1, Pallas kernels: 240 us -> 231 us  [local(): pl.pallas_call(functools.partial(mega, micro), out_shape=(jax.ShapeDtypeS...]
where the time goes in v3:
time: 238 us
  Pallas kernels  234 us (98%)
  local copies, waits for them, and re-layouts  2.83 us (1%)
    pallas_call x1, Pallas kernels, local(): pl.pallas_call(functools.partial(mega, micro), out_shape=(jax.ShapeDtypeS...  231 us

profile of v3, /device:TPU:1, one launch (start us, length us, event | category | flops | bytes accessed | tf_op | source)
XLA Modules:
  0.0 237.9 jit_solution(2442246641300335654)
XLA Ops:
  0.6 1.4 copy.12
  2.0 1.4 copy.13
  3.5 231.3 %shard_map.111 = (bf16[128,4096]{1,0:T(8,128)(2,1)}, bf16[512,768]{1,0:T(8,128)(2,1)}, bf16[512,768]{1,0:T(8,128)(2,1)}, bf16[512,768]{1,0:T(8,128)(2,1)}) custom-call(bf16[128,4096]{1,0:T(8,128)(2,1)} %bitcast.16, bf16[128,4096]{1,0:T(8,128)(2,1)} %bitcast.17, s32[128,2]{1,0:T(8,128)} %bitcast.11, f32[128,2]{1,0:T(8,128)} %bitcast.12, s32[1,8]{1,0:T(1,128)} %place_ref.1, ...), custom_call_target="tpu_custom_call" | custom-call | flops 20000000000 | bytes 24000000 | tf_op jit(solution)/shard_map/pallas_call | solution.py:490
  234.7 3.0 %shard_map.112 = (bf16[128,4096]{1,0:T(8,128)(2,1)}, bf16[512,768]{1,0:T(8,128)(2,1)}, bf16[512,768]{1,0:T(8,128)(2,1)}, bf16[512,768]{1,0:T(8,128)(2,1)}) custom-call(bf16[128,4096]{1,0:T(8,128)(2,1)} %get-tuple-element.12.refs_0_, bf16[512,768]{1,0:T(8,128)(2,1)} %get-tuple-element.13.refs_1_, bf16[512,768]{1,0:T(8,128)(2,1)} %get-tuple-element.14.refs_2_, ...), custom_call_target="tpu_custom_call" | custom-call | tf_op jit(solution)/shard_map/pallas_call | solution.py:536

commit v4 on v3

--- a/solution.py
+++ b/solution.py
@@ -8,6 +8,7 @@
 from jax.sharding import PartitionSpec as P
 
 CAP = 24
+RELAYED = 4
 NX = 4
 F32 = jnp.float32
 BF16 = jnp.bfloat16
@@ -25,9 +26,10 @@
     micro, x_ref, cot_ref, routes_ref, rw_ref, place_ref, wg_hbm, wu_hbm, wd_hbm,
     ig_ref, og_ref, ou_ref, od_ref,
     wg, wu, wd, xs, gs, xr, dr, ret, up, xsl, dsl, hh, aa, uu, yrecv,
-    sel, selt, scale, a_acc, u_acc, q_acc,
+    sel, selt, scale, rel, tab, sel1, scale1, a_acc, u_acc, q_acc,
     wsem, xss, xrs, gss, grs, dss, drs, lsem, pss, prs,
     xa_s, xa_r, da_s, da_r, h_s, h_r, ag_s, ag_r, au_s, au_r, ys, yr, igs, gos,
+    rls, rlr, fws, fwr, tbs, tbr,
 ):
     p = lax.axis_index("pipe")
     me = lax.axis_index("expert")
@@ -42,8 +44,8 @@
     rows = sel.shape[0]
     blk = rows // ne
     ff = wg.shape[2]
-    cw = d // NX
-    cp = cw // ny
+    nc = ndp
+    cp = d // nc
     is_last = p == last
 
     def at_z(e):
@@ -58,24 +60,19 @@
             device_id=dev, device_id_type=pl.DeviceIdType.MESH,
         )
 
+    def chunk(k):
+        return pl.ds(pl.multiple_of(k * cp, cp), cp)
+
     y_peer = (p, me, lax.rem(yh + 1, ny) * NX + x)
     p_peer = (last - p, me, j)
 
-    def w_copies(t, k):
+    def w_copy(t, k):
         src, dst = ((wg_hbm, wg), (wu_hbm, wu), (wd_hbm, wd))[t]
-        return [
-            pltpu.make_async_copy(
-                src.at[pl.ds(h * (d // ny) + k * cp, cp)],
-                dst.at[k, pl.ds(h * cp, cp)],
-                wsem.at[t, k, h],
-            )
-            for h in range(ny)
-        ]
+        return pltpu.make_async_copy(src.at[chunk(k)], dst.at[k], wsem.at[t, k])
 
     for t in range(3):
-        for k in range(NX):
-            for c in w_copies(t, k):
-                c.start()
+        for k in range(nc):
+            w_copy(t, k).start()
 
     barrier = pltpu.get_barrier_semaphore()
     peers = [at_z(lax.rem(me + o, ne)) for o in range(1, ne)]
@@ -89,36 +86,54 @@
     t_col = lax.broadcasted_iota(jnp.int32, square, 1)
     count = tokens // micro
     before = (t_col < t_row) & (t_col // count == t_row // count)
+    micro_of = (lax.broadcasted_iota(jnp.int32, (tokens, 1), 0) // count).astype(F32)
+
+    def as_row(column):
+        return jnp.transpose(jnp.broadcast_to(column, square))[0:1, :]
+
+    def tables(slots, weights, sel, scale):
+        by_row = [jnp.broadcast_to(slots[:, k : k + 1], square) for k in range(2)]
+        by_col = [jnp.transpose(v) for v in by_row]
+        places = []
+        for k in range(2):
+            same = jnp.where(by_col[0] == by_row[k], 1.0, 0.0) + jnp.where(
+                by_col[1] == by_row[k], 1.0, 0.0
+            )
+            rank = jnp.sum(jnp.where(before, same, 0.0), axis=1, keepdims=True)
+            places.append(slots[:, k : k + 1] * blk + micro_of * CAP + rank)
+        r_iota = lax.broadcasted_iota(jnp.int32, (rows, tokens), 0).astype(F32)
+        hits = [r_iota == as_row(v) for v in places]
+        sel[...] = jnp.where(hits[0] | hits[1], 1.0, 0.0).astype(BF16)
+        weight = sum(jnp.where(hits[k], as_row(weights[:, k : k + 1]), 0.0) for k in range(2))
+        scale[...] = jnp.broadcast_to(jnp.sum(weight, axis=1, keepdims=True), scale.shape)
+        return places
+
     ids = routes_ref[...]
     slots = jnp.zeros(ids.shape, jnp.int32)
     for s in range(ne):
         slots = jnp.where(ids == place_ref[0, s], s, slots)
     slots = slots.astype(F32)
-    by_row = [jnp.broadcast_to(slots[:, k : k + 1], square) for k in range(2)]
-    by_col = [jnp.transpose(v) for v in by_row]
-    micro_of = (lax.broadcasted_iota(jnp.int32, (tokens, 1), 0) // count).astype(F32)
-    places = []
-    for k in range(2):
-        same = jnp.where(by_col[0] == by_row[k], 1.0, 0.0) + jnp.where(
-            by_col[1] == by_row[k], 1.0, 0.0
-        )
-        rank = jnp.sum(jnp.where(before, same, 0.0), axis=1, keepdims=True)
-        places.append(slots[:, k : k + 1] * blk + micro_of * CAP + rank)
-
-    def as_row(column):
-        return jnp.transpose(jnp.broadcast_to(column, square))[0:1, :]
-
-    r_iota = lax.broadcasted_iota(jnp.int32, (rows, tokens), 0).astype(F32)
-    hits = [r_iota == as_row(v) for v in places]
-    sel[...] = jnp.where(hits[0] | hits[1], 1.0, 0.0).astype(BF16)
-    weight = sum(
-        jnp.where(hits[k], as_row(rw_ref[:, k : k + 1]), 0.0) for k in range(2)
-    )
-    scale[...] = jnp.broadcast_to(jnp.sum(weight, axis=1, keepdims=True), scale.shape)
+
+    @pl.when(is_last)
+    def _():
+        packed = jnp.zeros(tab.shape, F32)
+        lane = lax.broadcasted_iota(jnp.int32, tab.shape, 1)
+        for k in range(2):
+            packed = jnp.where(lane == k, slots[:, k : k + 1], packed)
+            packed = jnp.where(lane == 2 + k, rw_ref[:, k : k + 1], packed)
+        tab[...] = packed
+
+    tab_copy = mesh_copy(tab, tab, tbs.at[0], tbr.at[0], p_peer)
+
+    pl.semaphore_wait(barrier, len(peers))
+
+    @pl.when(is_last)
+    def _():
+        tab_copy.start()
+
+    places = tables(slots, rw_ref[...], sel, scale)
     c_iota = lax.broadcasted_iota(jnp.int32, (tokens, rows), 1).astype(F32)
     selt[...] = jnp.where((c_iota == places[0]) | (c_iota == places[1]), 1.0, 0.0).astype(BF16)
-
-    pl.semaphore_wait(barrier, len(peers))
 
     def my_rows(e):
         return pl.ds(pl.multiple_of(e * blk, 16), blk)
@@ -158,52 +173,110 @@
         for c in z_sends(stage, land, ss, rs, k):
             c.wait_send()
 
-    def piece(k, h):
-        return pl.ds(pl.multiple_of(h * (d // ny) + k * cp, cp), cp)
-
-    def chunk_of(ref, k):
-        return jnp.concatenate([ref[:, piece(k, h)] for h in range(ny)], axis=1)
-
     def send_scaled(k):
         picked = nn(sel[...], up[k])
         gs[k] = (scale[:, 0:1] * picked).astype(BF16)
         z_start(gs, dr, gss, grs, k)
 
     def turn(step):
-        return lax.rem(x + step, NX)
-
-    @pl.loop(0, NX)
+        own = step // (2 * NX - 2)
+        r = lax.rem(step, 3)
+        o = (1 - own) * (1 + 2 * r - 3 * (r // 2))
+        h = (1 - own) * (step // 3) + own * (step - (2 * NX - 2))
+        return h * NX + lax.rem(x + o, NX)
+
+    direct = nc - RELAYED
+
+    def relay_copy(m, o):
+        e = lax.rem(me + o, ne)
+        return mesh_copy(
+            gs.at[turn(direct + m), my_rows(e)], rel.at[m, my_rows(me)],
+            rls.at[m, o], rlr.at[m, o], at_z(e),
+        )
+
+    def relay_own(m):
+        return pltpu.make_async_copy(
+            gs.at[turn(direct + m), my_rows(me)], rel.at[m, my_rows(me)], rls.at[m, 0]
+        )
+
+    def hand_up(m):
+        return mesh_copy(rel.at[m], dr.at[turn(direct + m)], fws.at[m], fwr.at[m], p_peer)
+
+    def send_inputs(step):
+        k = turn(step)
+        xs[k] = nn(sel[...], x_ref[:, chunk(k)]).astype(BF16)
+        z_start(xs, xr, xss, xrs, k)
+
+        @pl.when(is_last)
+        def _():
+            up[k] = cot_ref[:, chunk(k)]
+
+        @pl.when(is_last & (step < direct))
+        def _():
+            send_scaled(k)
+
+    @pl.loop(0, 2)
     def _(step):
-        k = turn(step)
-        xs[k] = nn(sel[...], chunk_of(x_ref, k)).astype(BF16)
-        z_start(xs, xr, xss, xrs, k)
-
-        @pl.when(is_last)
-        def _():
-            up[k] = chunk_of(cot_ref, k)
-            send_scaled(k)
+        send_inputs(step)
+
+    @pl.when(jnp.logical_not(is_last))
+    def _():
+        tab_copy.wait_recv()
+        tables(tab[:, 0:2], tab[:, 2:4], sel1, scale1)
+
+        @pl.loop(0, RELAYED)
+        def _(m):
+            k = turn(direct + m)
+            picked = nn(sel1[...], cot_ref[:, chunk(k)])
+            gs[k] = (scale1[:, 0:1] * picked).astype(BF16)
+            for o in range(1, ne):
+                relay_copy(m, o).start()
+            relay_own(m).start()
+
+    @pl.loop(2, nc)
+    def _(step):
+        send_inputs(step)
+
+    @pl.when(jnp.logical_not(is_last))
+    def _():
+        @pl.loop(0, RELAYED)
+        def _(m):
+            for o in range(1, ne):
+                e = lax.rem(me + ne - o, ne)
+                mesh_copy(
+                    gs.at[turn(direct + m), my_rows(e)], rel.at[m, my_rows(e)],
+                    rls.at[m, o], rlr.at[m, o], at_z(e),
+                ).wait_recv()
+            relay_own(m).wait()
+            hand_up(m).start()
+            for o in range(1, ne):
+                relay_copy(m, o).wait_send()
 
     def share_copy(src, dst, ss, rs, k):
-        return mesh_copy(src.at[k], dst.at[x], ss.at[k], rs.at[x], at_x(k))
+        return mesh_copy(
+            src.at[k], dst.at[x, k // NX], ss.at[k], rs.at[x, k // NX], at_x(lax.rem(k, NX))
+        )
 
     def share_local(src, dst, k, n):
-        return pltpu.make_async_copy(src.at[k], dst.at[k], lsem.at[n])
+        return pltpu.make_async_copy(src.at[k], dst.at[x, k // NX], lsem.at[n, k // NX])
 
     def share_start(src, dst, ss, rs, k, n):
-        @pl.when(k != x)
+        @pl.when(lax.rem(k, NX) != x)
         def _():
             share_copy(src, dst, ss, rs, k).start()
 
-        @pl.when(k == x)
+        @pl.when(lax.rem(k, NX) == x)
         def _():
             share_local(src, dst, k, n).start()
 
     def share_wait(src, dst, ss, rs, n):
-        for o in range(1, NX):
-            k = lax.rem(x + o, NX)
-            share_copy(src, dst, ss, rs, k).wait_send()
-            mesh_copy(src.at[k], dst.at[k], ss.at[k], rs.at[k], at_x(k)).wait_recv()
-        share_local(src, dst, x, n).wait()
+        for h in range(ny):
+            for o in range(1, NX):
+                s = lax.rem(x + o, NX)
+                k = h * NX + s
+                share_copy(src, dst, ss, rs, k).wait_send()
+                mesh_copy(src.at[k], dst.at[s, h], ss.at[k], rs.at[s, h], at_x(s)).wait_recv()
+            share_local(src, dst, h * NX + x, n).wait()
 
     def rows_of(s):
         return pl.ds(pl.multiple_of(s * rows, 16), rows)
@@ -266,17 +339,13 @@
     u_acc[...] = jnp.zeros_like(u_acc)
     q_acc[...] = jnp.zeros_like(q_acc)
 
-    def wait_w(t, k):
-        for c in w_copies(t, k):
-            c.wait()
-
-    @pl.loop(0, NX)
+    @pl.loop(0, nc)
     def _(step):
         k = turn(step)
         z_recv(xs, xr, xss, xrs, k)
         share_start(xr, xsl, xa_s, xa_r, k, 0)
-        wait_w(0, k)
-        wait_w(1, k)
+        w_copy(0, k).wait()
+        w_copy(1, k).wait()
 
         @pl.loop(0, ff // tile)
         def _(n):
@@ -291,26 +360,36 @@
     def pipe_copy(k):
         return mesh_copy(up.at[k], up.at[k], pss.at[k], prs.at[k], p_peer)
 
-    def take_dr(k):
-        z_recv(gs, dr, gss, grs, k)
+    def take_dr(step):
+        k = turn(step)
+        relayed = is_last & (step >= direct)
+
+        @pl.when(relayed)
+        def _():
+            hand_up(step - direct).wait_recv()
+
+        @pl.when(jnp.logical_not(relayed))
+        def _():
+            z_recv(gs, dr, gss, grs, k)
+
         share_start(dr, dsl, da_s, da_r, k, 1)
-        wait_w(2, k)
+        w_copy(2, k).wait()
 
         @pl.loop(0, ff // tile)
         def _(n):
             c = pl.ds(pl.multiple_of(n * tile, tile), tile)
             q_acc[:, c] += nn(dr[k], wd[k, :, c])
 
-    @pl.loop(0, NX + 1)
+    @pl.loop(0, nc + 1)
     def _(step):
-        @pl.when(jnp.logical_not(is_last) & (step < NX))
+        @pl.when(jnp.logical_not(is_last) & (step < nc))
         def _():
             pipe_copy(turn(step)).wait_recv()
             send_scaled(turn(step))
 
         @pl.when(step > 0)
         def _():
-            take_dr(turn(step + NX - 1))
+            take_dr(step - 1)
 
     a = a_acc[...]
     sg = jax.nn.sigmoid(a)
@@ -322,32 +401,26 @@
     for n in range(pieces):
         ring_start(uu, au_s, au_r, n)
 
-    ct = 256 if cw % 256 == 0 else cw
-
-    @pl.loop(0, NX)
+
+    @pl.loop(0, nc)
     def _(step):
         k = turn(step)
         z_done(xs, xr, xss, xrs, k)
         ga = aa[rows_of(x), :]
         gu = uu[rows_of(x), :]
 
-        @pl.loop(0, cw // ct)
+        @pl.loop(0, cp // tile)
         def _(n):
-            c = pl.ds(pl.multiple_of(n * ct, ct), ct)
+            c = pl.ds(pl.multiple_of(n * tile, tile), tile)
             xs[k, :, c] = (nt(ga, wg[k, c, :]) + nt(gu, wu[k, c, :])).astype(BF16)
 
         z_start(xs, ret, dss, drs, k)
 
-    def ig_copies(k):
-        return [
-            pltpu.make_async_copy(
-                up.at[k, :, pl.ds(h * cp, cp)], ig_ref.at[:, piece(k, h)], igs.at[k, h]
-            )
-            for h in range(ny)
-        ]
+    def ig_copy(k):
+        return pltpu.make_async_copy(up.at[k], ig_ref.at[:, chunk(k)], igs.at[k])
 
     def combine():
-        @pl.loop(0, NX)
+        @pl.loop(0, nc)
         def _(step):
             k = turn(step)
             z_recv(xs, ret, dss, drs, k)
@@ -357,8 +430,7 @@
             def _():
                 pipe_copy(k).start()
 
-            for c in ig_copies(k):
-                c.start()
+            ig_copy(k).start()
 
     @pl.when(is_last)
     def _():
@@ -369,8 +441,8 @@
     def transposed(src, dst):
         for s in range(NX):
             for h in range(ny):
-                dst[s // kh, h * cp : (h + 1) * cp, (s % kh) * rows : (s % kh + 1) * rows] = (
-                    jnp.transpose(src[s, :, h * cp : (h + 1) * cp])
+                dst[s // kh * ny + h, :, (s % kh) * rows : (s % kh + 1) * rows] = (
+                    jnp.transpose(src[s, h])
                 )
 
     def columns(n):
@@ -378,32 +450,31 @@
 
     def product(lhs, rhs, h, n):
         c = columns(n)
-        r = pl.ds(pl.multiple_of(h * cp, cp), cp)
-        acc = nn(lhs[0, r, :], rhs[0 : kh * rows, c])
+        acc = nn(lhs[h], rhs[0 : kh * rows, c])
         for m in range(1, NX // kh):
-            acc += nn(lhs[m, r, :], rhs[m * kh * rows : (m + 1) * kh * rows, c])
+            acc += nn(lhs[m * ny + h], rhs[m * kh * rows : (m + 1) * kh * rows, c])
         return acc
 
     def y_copy(t, n):
         return mesh_copy(
-            wd.at[t, pl.ds(0, cp), columns(n)], yrecv.at[t, :, columns(n)],
+            wd.at[t, :, columns(n)], yrecv.at[t, :, columns(n)],
             ys.at[t, n], yr.at[t, n], y_peer,
         )
 
     def for_peer(t, lhs, rhs, n):
-        wd[t, 0:cp, columns(n)] = product(lhs, rhs, lax.rem(yh + 1, ny), n).astype(BF16)
+        wd[t, :, columns(n)] = product(lhs, rhs, lax.rem(yh + 1, ny), n).astype(BF16)
         y_copy(t, n).start()
 
     def out_copy(t, n):
         out = (od_ref, og_ref, ou_ref)[t]
         return pltpu.make_async_copy(
-            wd.at[t, pl.ds(cp, cp), columns(n)], out.at[:, columns(n)], gos.at[t, n]
+            wd.at[3 + t, :, columns(n)], out.at[:, columns(n)], gos.at[t, n]
         )
 
     def for_me(t, lhs, rhs, n):
         mine = product(lhs, rhs, yh, n)
         y_copy(t, n).wait()
-        wd[t, cp : 2 * cp, columns(n)] = (
+        wd[3 + t, :, columns(n)] = (
             mine + yrecv[t, :, columns(n)].astype(F32)
         ).astype(BF16)
         out_copy(t, n).start()
@@ -437,16 +508,30 @@
     for args in ring:
         ring_done(*args)
 
-    @pl.loop(0, NX)
-    def _(k):
-        z_done(gs, dr, gss, grs, k)
+    @pl.loop(0, nc)
+    def _(step):
+        k = turn(step)
+
+        @pl.when(jnp.logical_not(is_last) | (step < direct))
+        def _():
+            z_done(gs, dr, gss, grs, k)
+
         z_done(xs, ret, dss, drs, k)
-        for c in ig_copies(k):
-            c.wait()
+        ig_copy(k).wait()
 
         @pl.when(is_last)
         def _():
             pipe_copy(k).wait_send()
+
+    @pl.when(is_last)
+    def _():
+        tab_copy.wait_send()
+
+    @pl.when(jnp.logical_not(is_last))
+    def _():
+        @pl.loop(0, RELAYED)
+        def _(m):
+            hand_up(m).wait_send()
 
     for t in range(3):
         for n in range(pieces):
@@ -477,14 +562,15 @@
     tokens = micro * count
     ff = gate_weight.shape[3]
     rows = ne * micro * CAP
-    cw = d // NX
-    cp = cw // ny
+    nc = NX * ny
+    cp = d // nc
     vm = functools.partial(pl.BlockSpec, memory_space=pltpu.VMEM)
     hbm = functools.partial(pl.BlockSpec, memory_space=pl.ANY)
     dma = pltpu.SemaphoreType.DMA
-    wide = pltpu.VMEM((NX, rows, cw), BF16)
+    wide = pltpu.VMEM((nc, rows, cp), BF16)
+    shares = pltpu.VMEM((NX, ny, rows, cp), BF16)
     tall = pltpu.VMEM((NX * rows, ff), BF16)
-    weight = pltpu.VMEM((NX, cw, ff), BF16)
+    weight = pltpu.VMEM((nc, cp, ff), BF16)
     acc = pltpu.VMEM((rows, ff), F32)
     np_ = ff // 256
     outs = pl.pallas_call(
@@ -500,22 +586,28 @@
         scratch_shapes=[
             weight, weight, weight,
             wide, wide, wide, wide, wide,
-            pltpu.VMEM((NX, tokens, cw), BF16),
-            wide, wide,
+            pltpu.VMEM((nc, tokens, cp), BF16),
+            shares, shares,
             tall, tall, tall,
             pltpu.VMEM((3, cp, ff), BF16),
             pltpu.VMEM((rows, tokens), BF16),
             pltpu.VMEM((tokens, rows), BF16),
             pltpu.VMEM((rows, 128), F32),
+            pltpu.VMEM((RELAYED, rows, cp), BF16),
+            pltpu.VMEM((tokens, 128), F32),
+            pltpu.VMEM((rows, tokens), BF16),
+            pltpu.VMEM((rows, 128), F32),
             acc, acc, acc,
-            dma((3, NX, ny)),
-            dma((NX, ne)), dma((NX, ne)), dma((NX, ne)), dma((NX, ne)),
-            dma((NX, ne)), dma((NX, ne)),
-            dma((2,)),
-            dma((NX,)), dma((NX,)),
-            dma((NX,)), dma((NX,)), dma((NX,)), dma((NX,)),
+            dma((3, nc)),
+            dma((nc, ne)), dma((nc, ne)), dma((nc, ne)), dma((nc, ne)),
+            dma((nc, ne)), dma((nc, ne)),
+            dma((2, ny)),
+            dma((nc,)), dma((nc,)),
+            dma((nc,)), dma((NX, ny)), dma((nc,)), dma((NX, ny)),
             dma((NX,)), dma((NX,)), dma((np_, 4)), dma((np_, 4)), dma((np_, 4)), dma((np_, 4)),
-            dma((3, np_)), dma((3, np_)), dma((NX, ny)), dma((3, np_)),
+            dma((3, np_)), dma((3, np_)), dma((nc,)), dma((3, np_)),
+            dma((RELAYED, ne)), dma((RELAYED, ne)), dma((RELAYED,)), dma((RELAYED,)),
+            dma((1,)), dma((1,)),
         ],
         compiler_params=pltpu.CompilerParams(
             collective_id=0, has_side_effects=True, vmem_limit_bytes=63 * 2**20

time: 238 us -> 213 us (0.89)
  Pallas kernels: 234 us -> 209 us
    pallas_call x1, Pallas kernels: 231 us -> 206 us  [local(): pl.pallas_call(functools.partial(mega, micro), out_shape=(jax.ShapeDtypeS...]
where the time goes in v4:
time: 213 us
  Pallas kernels  209 us (98%)
  local copies, waits for them, and re-layouts  2.83 us (1%)
    pallas_call x1, Pallas kernels, local(): pl.pallas_call(functools.partial(mega, micro), out_shape=(jax.ShapeDtypeS...  206 us

profile of v4, /device:TPU:1, one launch (start us, length us, event | category | flops | bytes accessed | tf_op | source)
XLA Modules:
  0.0 212.6 jit_solution(14154539444938248719)
XLA Ops:
  0.6 1.4 copy.12
  2.0 1.4 copy.13
  3.5 206.0 %shard_map.111 = (bf16[128,4096]{1,0:T(8,128)(2,1)}, bf16[512,768]{1,0:T(8,128)(2,1)}, bf16[512,768]{1,0:T(8,128)(2,1)}, bf16[512,768]{1,0:T(8,128)(2,1)}) custom-call(bf16[128,4096]{1,0:T(8,128)(2,1)} %bitcast.16, bf16[128,4096]{1,0:T(8,128)(2,1)} %bitcast.17, s32[128,2]{1,0:T(8,128)} %bitcast.11, f32[128,2]{1,0:T(8,128)} %bitcast.12, s32[1,8]{1,0:T(1,128)} %place_ref.1, ...), custom_call_target="tpu_custom_call" | custom-call | flops 20000000000 | bytes 24000000 | tf_op jit(solution)/shard_map/pallas_call | solution.py:576
  209.4 3.0 %shard_map.112 = (bf16[128,4096]{1,0:T(8,128)(2,1)}, bf16[512,768]{1,0:T(8,128)(2,1)}, bf16[512,768]{1,0:T(8,128)(2,1)}, bf16[512,768]{1,0:T(8,128)(2,1)}) custom-call(bf16[128,4096]{1,0:T(8,128)(2,1)} %get-tuple-element.12.refs_0_, bf16[512,768]{1,0:T(8,128)(2,1)} %get-tuple-element.13.refs_1_, bf16[512,768]{1,0:T(8,128)(2,1)} %get-tuple-element.14.refs_2_, ...), custom_call_target="tpu_custom_call" | custom-call | tf_op jit(solution)/shard_map/pallas_call | solution.py:628

commit v5 on v4

--- a/solution.py
+++ b/solution.py
@@ -92,35 +92,40 @@
         return jnp.transpose(jnp.broadcast_to(column, square))[0:1, :]
 
     def tables(slots, weights, sel, scale):
-        by_row = [jnp.broadcast_to(slots[:, k : k + 1], square) for k in range(2)]
-        by_col = [jnp.transpose(v) for v in by_row]
+        by_col = [jnp.broadcast_to(slots[k], square) for k in range(2)]
+        by_row = [jnp.transpose(v) for v in by_col]
         places = []
         for k in range(2):
             same = jnp.where(by_col[0] == by_row[k], 1.0, 0.0) + jnp.where(
                 by_col[1] == by_row[k], 1.0, 0.0
             )
             rank = jnp.sum(jnp.where(before, same, 0.0), axis=1, keepdims=True)
-            places.append(slots[:, k : k + 1] * blk + micro_of * CAP + rank)
+            places.append(by_row[k][:, 0:1] * blk + micro_of * CAP + rank)
         r_iota = lax.broadcasted_iota(jnp.int32, (rows, tokens), 0).astype(F32)
         hits = [r_iota == as_row(v) for v in places]
         sel[...] = jnp.where(hits[0] | hits[1], 1.0, 0.0).astype(BF16)
-        weight = sum(jnp.where(hits[k], as_row(weights[:, k : k + 1]), 0.0) for k in range(2))
+        weight = sum(jnp.where(hits[k], weights[k], 0.0) for k in range(2))
         scale[...] = jnp.broadcast_to(jnp.sum(weight, axis=1, keepdims=True), scale.shape)
         return places
 
-    ids = routes_ref[...]
-    slots = jnp.zeros(ids.shape, jnp.int32)
-    for s in range(ne):
-        slots = jnp.where(ids == place_ref[0, s], s, slots)
-    slots = slots.astype(F32)
+    def in_row(ref, k):
+        return jnp.concatenate([ref[k, m : m + 1, :] for m in range(micro)], axis=1)
+
+    slots, weights = [], []
+    for k in range(2):
+        ids = in_row(routes_ref, k)
+        slot = jnp.zeros(ids.shape, jnp.int32)
+        for s in range(ne):
+            slot = jnp.where(ids == place_ref[0, s], s, slot)
+        slots.append(slot.astype(F32))
+        weights.append(in_row(rw_ref, k))
 
     @pl.when(is_last)
     def _():
         packed = jnp.zeros(tab.shape, F32)
-        lane = lax.broadcasted_iota(jnp.int32, tab.shape, 1)
-        for k in range(2):
-            packed = jnp.where(lane == k, slots[:, k : k + 1], packed)
-            packed = jnp.where(lane == 2 + k, rw_ref[:, k : k + 1], packed)
+        line = lax.broadcasted_iota(jnp.int32, tab.shape, 0)
+        for n, row in enumerate(slots + weights):
+            packed = jnp.where(line == n, row, packed)
         tab[...] = packed
 
     tab_copy = mesh_copy(tab, tab, tbs.at[0], tbr.at[0], p_peer)
@@ -131,7 +136,7 @@
     def _():
         tab_copy.start()
 
-    places = tables(slots, rw_ref[...], sel, scale)
+    places = tables(slots, weights, sel, scale)
     c_iota = lax.broadcasted_iota(jnp.int32, (tokens, rows), 1).astype(F32)
     selt[...] = jnp.where((c_iota == places[0]) | (c_iota == places[1]), 1.0, 0.0).astype(BF16)
 
@@ -222,7 +227,8 @@
     @pl.when(jnp.logical_not(is_last))
     def _():
         tab_copy.wait_recv()
-        tables(tab[:, 0:2], tab[:, 2:4], sel1, scale1)
+        held = [tab[n : n + 1, :] for n in range(4)]
+        tables(held[0:2], held[2:4], sel1, scale1)
 
         @pl.loop(0, RELAYED)
         def _(m):
@@ -448,22 +454,26 @@
     def columns(n):
         return pl.ds(n * tile, tile)
 
-    def product(lhs, rhs, h, n):
+    def part(v):
+        return pl.ds(v * (cp // 2), cp // 2)
+
+    def product(lhs, rhs, h, n, v):
         c = columns(n)
-        acc = nn(lhs[h], rhs[0 : kh * rows, c])
+        acc = nn(lhs[h, part(v)], rhs[0 : kh * rows, c])
         for m in range(1, NX // kh):
-            acc += nn(lhs[m * ny + h], rhs[m * kh * rows : (m + 1) * kh * rows, c])
+            acc += nn(lhs[m * ny + h, part(v)], rhs[m * kh * rows : (m + 1) * kh * rows, c])
         return acc
 
-    def y_copy(t, n):
+    def y_copy(t, n, v):
         return mesh_copy(
-            wd.at[t, :, columns(n)], yrecv.at[t, :, columns(n)],
-            ys.at[t, n], yr.at[t, n], y_peer,
+            wd.at[t, part(v), columns(n)], yrecv.at[t, part(v), columns(n)],
+            ys.at[t, 2 * n + v], yr.at[t, 2 * n + v], y_peer,
         )
 
     def for_peer(t, lhs, rhs, n):
-        wd[t, :, columns(n)] = product(lhs, rhs, lax.rem(yh + 1, ny), n).astype(BF16)
-        y_copy(t, n).start()
+        for v in range(2):
+            wd[t, part(v), columns(n)] = product(lhs, rhs, lax.rem(yh + 1, ny), n, v).astype(BF16)
+            y_copy(t, n, v).start()
 
     def out_copy(t, n):
         out = (od_ref, og_ref, ou_ref)[t]
@@ -472,11 +482,12 @@
         )
 
     def for_me(t, lhs, rhs, n):
-        mine = product(lhs, rhs, yh, n)
-        y_copy(t, n).wait()
-        wd[3 + t, :, columns(n)] = (
-            mine + yrecv[t, :, columns(n)].astype(F32)
-        ).astype(BF16)
+        for v in range(2):
+            mine = product(lhs, rhs, yh, n, v)
+            y_copy(t, n, v).wait()
+            wd[3 + t, part(v), columns(n)] = (
+                mine + yrecv[t, part(v), columns(n)].astype(F32)
+            ).astype(BF16)
         out_copy(t, n).start()
 
     ring = [(aa, ag_s, ag_r, n) for n in range(pieces)]
@@ -594,7 +605,7 @@
             pltpu.VMEM((tokens, rows), BF16),
             pltpu.VMEM((rows, 128), F32),
             pltpu.VMEM((RELAYED, rows, cp), BF16),
-            pltpu.VMEM((tokens, 128), F32),
+            pltpu.VMEM((8, tokens), F32),
             pltpu.VMEM((rows, tokens), BF16),
             pltpu.VMEM((rows, 128), F32),
             acc, acc, acc,
@@ -605,7 +616,7 @@
             dma((nc,)), dma((nc,)),
             dma((nc,)), dma((NX, ny)), dma((nc,)), dma((NX, ny)),
             dma((NX,)), dma((NX,)), dma((np_, 4)), dma((np_, 4)), dma((np_, 4)), dma((np_, 4)),
-            dma((3, np_)), dma((3, np_)), dma((nc,)), dma((3, np_)),
+            dma((3, 2 * np_)), dma((3, 2 * np_)), dma((nc,)), dma((3, np_)),
             dma((RELAYED, ne)), dma((RELAYED, ne)), dma((RELAYED,)), dma((RELAYED,)),
             dma((1,)), dma((1,)),
         ],
@@ -618,8 +629,8 @@
     )(
         activations.reshape(tokens, d),
         cotangent.reshape(tokens, d),
-        routes.reshape(tokens, -1),
-        route_weights.reshape(tokens, -1),
+        jnp.transpose(routes[0], (2, 0, 1)),
+        jnp.transpose(route_weights[0], (2, 0, 1)),
         placement,
         gate_weight[0, 0],
         up_weight[0, 0],

time: 213 us -> 212 us (level)
  no operation moved by 1% of the time
where the time goes in v5:
time: 212 us
  Pallas kernels  209 us (99%)
  local copies, waits for them, and re-layouts  2.52 us (1%)
    pallas_call x1, Pallas kernels, local(): pl.pallas_call(functools.partial(mega, micro), out_shape=(jax.ShapeDtypeS...  206 us

profile of v5, /device:TPU:1, one launch (start us, length us, event | category | flops | bytes accessed | tf_op | source)
XLA Modules:
  0.0 211.9 jit_solution(10107714822839901071)
XLA Ops:
  0.6 1.3 copy.17
  1.9 1.3 copy.16
  3.2 205.6 %shard_map.111 = (bf16[128,4096]{1,0:T(8,128)(2,1)}, bf16[512,768]{1,0:T(8,128)(2,1)}, bf16[512,768]{1,0:T(8,128)(2,1)}, bf16[512,768]{1,0:T(8,128)(2,1)}) custom-call(bf16[128,4096]{1,0:T(8,128)(2,1)} %bitcast.24, bf16[128,4096]{1,0:T(8,128)(2,1)} %bitcast.25, s32[2,2,64]{2,1,0:T(2,128)} %bitcast.19, f32[2,2,64]{2,1,0:T(2,128)} %bitcast.20, ...), custom_call_target="tpu_custom_call" | custom-call | flops 20000000000 | bytes 24000000 | tf_op jit(solution)/shard_map/pallas_call | solution.py:587
  208.7 3.0 %shard_map.112 = (bf16[128,4096]{1,0:T(8,128)(2,1)}, bf16[512,768]{1,0:T(8,128)(2,1)}, bf16[512,768]{1,0:T(8,128)(2,1)}, bf16[512,768]{1,0:T(8,128)(2,1)}) custom-call(bf16[128,4096]{1,0:T(8,128)(2,1)} %get-tuple-element.12.refs_0_, bf16[512,768]{1,0:T(8,128)(2,1)} %get-tuple-element.13.refs_1_, bf16[512,768]{1,0:T(8,128)(2,1)} %get-tuple-element.14.refs_2_, ...), custom_call_target="tpu_custom_call" | custom-call | tf_op jit(solution)/shard_map/pallas_call | solution.py:639
